TPU v7x, 128 devices: a whole 4x4x4 slice. The times are simulated.
128 devices in a mesh: shot: 8 (over y, z_hi), gx: 16 (over z_lo, x, core).
Axes of the slice: x: 4, y: 4, z: 4 (z_hi: 2, z_lo: 2; z = z_hi * 2 + z_lo), core: 2. Of those that a mesh axis runs over, the one named last changes fastest.
Arguments:
- courant: float32 [128, 64, 256], P('gx'), may hold values from 0.08 to 0.3
- absorb: int32 [6], replicated, may hold values from 4 to 11
- model_image: float32 [128, 64, 256], P('gx'), may hold values from -6 to 6
- direction: float32 [128, 64, 256], P('gx'), may hold values from -6 to 6
- back_prev: float32 [16, 128, 64, 256], P('shot', 'gx'), may hold values from -12 to 12
- back_now: float32 [16, 128, 64, 256], P('shot', 'gx'), may hold values from -12 to 12
- scat_prev: float32 [16, 128, 64, 256], P('shot', 'gx'), may hold values from -12 to 12
- scat_now: float32 [16, 128, 64, 256], P('shot', 'gx'), may hold values from -12 to 12
- back_end: float32 [16, 128, 64, 256], P('shot', 'gx'), may hold values from -12 to 12
- back_before_end: float32 [16, 128, 64, 256], P('shot', 'gx'), may hold values from -12 to 12
- back_band: float32 [16, 4, 128, 64, 256], P('shot', None, 'gx'), may hold values from -12 to 12
- src_pos: int32 [16, 64, 3], P('shot'), may hold values from 0 to 255, as said below
- wavelet: float32 [16, 4], P('shot'), may hold values from -30 to 30
- rec_pos: int32 [16, 2048, 3], P('shot', 'gx'), may hold values from 0 to 255, as said below
- residual: float32 [16, 4, 2048], P('shot', None, 'gx'), may hold values from -6 to 6
- grad_norm: float32 [1], replicated, may hold values from 131072 to 786432
Outputs:
- image_new: float32 [128, 64, 256], P('gx')
- direction_new: float32 [128, 64, 256], P('gx')
- residual_new: float32 [16, 4, 2048], P('shot', None, 'gx')
Inputs may be any that keep to these rules, and one draw needn't show every extreme that they name: `src_pos`: each entry is a grid cell: 0 <= x < 128, 0 <= y < 64, 0 <= z < 256. Each entry is a grid cell with 0 <= y < 64 and 0 <= z < 256; receiver j lies at an x between (j // 128) * 8 and (j // 128) * 8 + 7; every shot group uses the same receiver cells (rec_pos[s] is the same for every s).
All inputs are finite; a program needn't handle non-finite values.
Results may differ from a plain program's by a relative error of at most 0.00027.
Values sent between devices are 32-bit elements; how exact they have to be, the bound alone decides.
A program may use at most 128 MiB of HBM per device.

v0:
```python
import functools

import jax
import jax.numpy as jnp
from jax import lax
from jax.experimental import pallas as pl
from jax.experimental.pallas import tpu as pltpu
from jax.sharding import PartitionSpec as P

damp_peak = 0.4
tiny = 1e-6
CX, NY, NZ = 8, 64, 256
NS, STEPS, REC, SRC = 2, 4, 128, 64
PY = 80
HALF = 128
MESH = pl.DeviceIdType.MESH
f32 = jnp.float32
bf16 = jnp.bfloat16


def split2(v):
    hi = v.astype(bf16)
    lo = (v - hi.astype(f32)).astype(bf16)
    return hi, lo


def profile(pos, extent, low, high):
    gap = extent - 1 - pos
    low_f = low.astype(f32)
    high_f = high.astype(f32)
    near_low = jnp.where(pos < low, ((low - pos).astype(f32) / low_f) ** 2, 0.0)
    near_high = jnp.where(gap < high, ((high - gap).astype(f32) / high_f) ** 2, 0.0)
    return damp_peak * (near_low + near_high)


def kernel(
    n_shot,
    n_gx,
    courant_h,
    direction_h,
    back_prev_h,
    back_now_h,
    scat_prev_h,
    scat_now_h,
    back_end_h,
    back_before_h,
    band_h,
    absorb,
    wavelet,
    grad_norm,
    src_pos,
    rec_pos,
    residual,
    grad_o,
    resid_o,
    scal_o,
    F0,
    F1,
    U0,
    U1,
    band,
    c0,
    dirv,
    ca,
    cb,
    cc,
    inv,
    cnt,
    rowhot,
    zt,
    zh2,
    tr,
    amt,
    img,
    rs,
    ebuf,
    eslot_s,
    eslot_g,
    ld_sem,
    f_send,
    f_recv,
    u_send,
    u_recv,
    e_send_s,
    e_recv_s,
    e_send_g,
    e_recv_g,
    g_send,
    g_recv,
):
    me_s = lax.axis_index("shot")
    me_g = lax.axis_index("gx")
    F = (F0, F1)
    U = (U0, U1)

    loads = {}

    def load(name, src, dst, k):
        c = pltpu.make_async_copy(src, dst, ld_sem.at[k])
        c.start()
        loads.setdefault(name, []).append(c)

    k = 0
    for z in range(2):
        zs = pl.ds(z * HALF, HALF)
        load("coef", courant_h.at[:, :, zs], c0.at[z], k)
        k += 1
    fields = (
        ("f0", 0, 0, back_now_h),
        ("f0", 0, 1, scat_now_h),
        ("f0", 0, 2, back_before_h),
        ("f1", 1, 0, back_prev_h),
        ("f1", 1, 1, scat_prev_h),
        ("f1", 1, 2, back_end_h),
    )
    for name, b, f, src in fields:
        for z in range(2):
            zs = pl.ds(z * HALF, HALF)
            load(
                name,
                src.at[:, :, :, zs],
                F[b].at[f, :, z, pl.ds(1, CX), pl.ds(8, NY), :],
                k,
            )
            k += 1
    for z in range(2):
        zs = pl.ds(z * HALF, HALF)
        load("f1", direction_h.at[:, :, zs], dirv.at[z], k)
        k += 1
    load("f1", band_h, band, k)

    zero8 = jnp.zeros((8, HALF), f32)
    zero64 = jnp.zeros((NY, HALF), f32)

    def zero_pads(ref, lead):
        def one(p, carry):
            for idx in lead:
                ref[idx + (p, pl.ds(0, 8), slice(None))] = zero8
                ref[idx + (p, pl.ds(72, 8), slice(None))] = zero8
            return carry

        lax.fori_loop(0, CX + 2, one, 0)
        for idx in lead:
            for p in (0, CX + 1):
                ref[idx + (p, pl.ds(8, NY), slice(None))] = zero64

    lead3 = [(f, s, z) for f in range(3) for s in range(NS) for z in range(2)]
    lead2 = [(s, z) for s in range(NS) for z in range(2)]
    for b in range(2):
        zero_pads(F[b], lead3)
        zero_pads(U[b], lead2)

    bar = pltpu.get_barrier_semaphore()
    for d in range(1, n_gx):
        pl.semaphore_signal(
            bar, inc=1, device_id=(me_s, lax.rem(me_g + d, n_gx)), device_id_type=MESH
        )
    for d in range(1, n_shot):
        pl.semaphore_signal(
            bar, inc=1, device_id=(lax.rem(me_s + d, n_shot), me_g), device_id_type=MESH
        )
    pl.semaphore_wait(bar, n_gx - 1 + n_shot - 1)

    def face(buf, lead, send, recv, side):
        src_p, dst_p = (1, CX + 1) if side == 0 else (CX, 0)
        nb = me_g - 1 if side == 0 else me_g + 1
        return pltpu.make_async_remote_copy(
            src_ref=buf.at[lead + (src_p, pl.ds(8, NY), slice(None))],
            dst_ref=buf.at[lead + (dst_p, pl.ds(8, NY), slice(None))],
            send_sem=send.at[side],
            recv_sem=recv.at[side],
            device_id=(me_s, nb),
            device_id_type=MESH,
        )

    has_left = me_g > 0
    has_right = me_g < n_gx - 1

    def send_faces(buf, lead, send, recv):
        @pl.when(has_left)
        def _():
            face(buf, lead, send, recv, 0).start()

        @pl.when(has_right)
        def _():
            face(buf, lead, send, recv, 1).start()

    def wait_recv(buf, lead, send, recv):
        @pl.when(has_right)
        def _():
            face(buf, lead, send, recv, 0).wait_recv()

        @pl.when(has_left)
        def _():
            face(buf, lead, send, recv, 1).wait_recv()

    def wait_send(buf, lead, send, recv):
        @pl.when(has_left)
        def _():
            face(buf, lead, send, recv, 0).wait_send()

        @pl.when(has_right)
        def _():
            face(buf, lead, send, recv, 1).wait_send()

    all3 = (slice(None), slice(None), slice(None))
    all2 = (slice(None), slice(None))

    for c in loads["f0"]:
        c.wait()
    send_faces(F0, all3, f_send.at[0], f_recv.at[0])

    lane128 = lax.broadcasted_iota(jnp.int32, (REC, REC), 1)
    sub128 = lax.broadcasted_iota(jnp.int32, (REC, REC), 0)

    def to_row(col, n):
        eye = (
            lax.broadcasted_iota(jnp.int32, (n, n), 0)
            == lax.broadcasted_iota(jnp.int32, (n, n), 1)
        )
        return jnp.sum(jnp.where(eye, col.astype(f32), 0.0), axis=0, keepdims=True)

    rec = rec_pos[0]
    rec_row_col = (rec[:, 0:1] - me_g * CX) * NY + rec[:, 1:2]
    rec_z_col = rec[:, 2:3]
    rec_row = to_row(rec_row_col, REC).astype(jnp.int32)
    rec_z = to_row(rec_z_col, REC).astype(jnp.int32)
    rowhot[...] = jnp.where(
        lax.broadcasted_iota(jnp.int32, (CX * NY, REC), 0) == rec_row, 1.0, 0.0
    )
    zt[...] = jnp.where(
        lax.broadcasted_iota(jnp.int32, (NZ, REC), 0) == rec_z, 1.0, 0.0
    ).astype(bf16)
    zhot = jnp.where(
        lax.broadcasted_iota(jnp.int32, (REC, NZ), 1) == rec_z_col, 1.0, 0.0
    ).astype(bf16)
    zh2[pl.ds(0, REC), :] = zhot
    zh2[pl.ds(REC, REC), :] = zhot

    for c in loads["coef"]:
        c.wait()

    nx = n_gx * CX
    damp_z = [
        profile(
            lax.broadcasted_iota(jnp.int32, (8, HALF), 1) + z * HALF, NZ, absorb[4], absorb[5]
        )
        for z in range(2)
    ]

    def coef(i, carry):
        p = i // 8
        y8 = pl.multiple_of((i % 8) * 8, 8)
        ys = pl.ds(y8, 8)
        pos_x = jnp.full((8, HALF), me_g * CX + p, jnp.int32)
        damp_xy = profile(pos_x, nx, absorb[0], absorb[1]) + profile(
            lax.broadcasted_iota(jnp.int32, (8, HALF), 0) + y8, NY, absorb[2], absorb[3]
        )
        for z in range(2):
            damping = damp_xy + damp_z[z]
            c = c0[z, p, ys, :]
            iv = 1.0 / (1.0 + damping)
            inv[z, p, ys, :] = iv
            ca[z, p, ys, :] = (2.0 - 6.0 * c) * iv
            cb[z, p, ys, :] = (1.0 - damping) * iv
            cc[z, p, ys, :] = c * iv
        return carry

    lax.fori_loop(0, CX * 8, coef, 0)

    for s in range(NS):
        src = src_pos[s]
        s_row = to_row((src[:, 0:1] - me_g * CX) * NY + src[:, 1:2], SRC).astype(jnp.int32)
        s_zhot = jnp.where(
            lax.broadcasted_iota(jnp.int32, (SRC, NZ), 1) == src[:, 2:3], 1.0, 0.0
        ).astype(bf16)

        def count(p, carry):
            rows = lax.broadcasted_iota(jnp.int32, (NY, SRC), 0) + p * NY
            hot = jnp.where(rows == s_row, 1.0, 0.0).astype(bf16)
            n = jnp.dot(hot, s_zhot, preferred_element_type=f32)
            for z in range(2):
                cnt[s, z, p] = n[:, z * HALF : (z + 1) * HALF] * inv[z, p]
            return carry

        lax.fori_loop(0, CX, count, 0)

    for c in loads["f1"]:
        c.wait()

    lane = lax.broadcasted_iota(jnp.int32, (8, HALF), 1)
    first = lane == 0
    last = lane == HALF - 1

    def neighbours(ref, lead, p, y8):
        ys = pl.ds(pl.multiple_of(y8 + 8, 8), 8)
        mid = [ref[lead + (z, p, ys, slice(None))] for z in range(2)]
        sums = []
        right = [pltpu.roll(m, 1, 1) for m in mid]
        left = [pltpu.roll(m, HALF - 1, 1) for m in mid]
        low = [jnp.where(first, 0.0, right[0]), jnp.where(first, right[0], right[1])]
        high = [jnp.where(last, left[1], left[0]), jnp.where(last, 0.0, left[1])]
        for z in range(2):
            t = ref[lead + (z, p + 1, ys, slice(None))] + ref[lead + (z, p - 1, ys, slice(None))]
            t = t + (
                ref[lead + (z, p, pl.ds(y8 + 9, 8), slice(None))]
                + ref[lead + (z, p, pl.ds(y8 + 7, 8), slice(None))]
            )
            sums.append(t + (low[z] + high[z]))
        return mid, sums

    def forward(n, p, y8):
        now, nxt = F[n % 2], F[(n + 1) % 2]
        q = p - 1
        ys = pl.ds(y8, 8)
        ysp = pl.ds(pl.multiple_of(y8 + 8, 8), 8)
        a = [ca[z, q, ys, :] for z in range(2)]
        b = [cb[z, q, ys, :] for z in range(2)]
        c = [cc[z, q, ys, :] for z in range(2)]
        cr = [c0[z, q, ys, :] for z in range(2)]
        di = [dirv[z, q, ys, :] for z in range(2)]
        for s in range(NS):
            k = [cnt[s, z, q, ys, :] for z in range(2)]
            w = wavelet[s, n]
            wr = wavelet[s, STEPS - 1 - n]
            mid, sums = neighbours(now, (0, s), p, y8)
            acc = []
            for z in range(2):
                old = nxt[0, s, z, p, ysp, :]
                new = a[z] * mid[z] - b[z] * old + c[z] * sums[z] + w * k[z]
                nxt[0, s, z, p, ysp, :] = new
                acc.append((new - mid[z]) - (mid[z] - old))
            mid, sums = neighbours(now, (1, s), p, y8)
            for z in range(2):
                old = nxt[1, s, z, p, ysp, :]
                nxt[1, s, z, p, ysp, :] = (
                    a[z] * mid[z] - b[z] * old + c[z] * (sums[z] - di[z] * acc[z])
                )
            mid, sums = neighbours(now, (2, s), p, y8)
            for z in range(2):
                zs = pl.ds(z * HALF, HALF)
                old = nxt[2, s, z, p, ysp, :]
                new = a[z] * mid[z] - b[z] * old + c[z] * sums[z] + wr * k[z]
                kept = band[s, STEPS - 1 - n, q, ys, zs]
                new = jnp.where(b[z] < 1.0, kept, new)
                nxt[2, s, z, p, ysp, :] = new
                band[s, STEPS - 1 - n, q, ys, zs] = cr[z] * ((new - mid[z]) - (mid[z] - old))

    def gather(n):
        ref = F[(n + 1) % 2]
        zero = jnp.zeros((NY, REC), f32)

        def one(p, carry):
            hot = rowhot[pl.ds(pl.multiple_of(p * NY, NY), NY), :]
            out = []
            for s in range(NS):
                v = jnp.concatenate(
                    [ref[1, s, z, p + 1, pl.ds(8, NY), :] for z in range(2)], axis=1
                )
                hi, lo = split2(v)
                g = jnp.dot(hi, zt[...], preferred_element_type=f32) + jnp.dot(
                    lo, zt[...], preferred_element_type=f32
                )
                out.append(carry[s] + hot * g)
            return tuple(out)

        got = lax.fori_loop(0, CX, one, (zero, zero))
        for s in range(NS):
            tr[pl.ds(s * STEPS + n, 1), :] = jnp.sum(got[s], axis=0, keepdims=True)

    for n in range(STEPS):
        wait_recv(F[n % 2], all3, f_send.at[n], f_recv.at[n])
        if n > 0:
            wait_send(F[(n + 1) % 2], all3, f_send.at[n - 1], f_recv.at[n - 1])

        def edge(i, carry):
            forward(n, 1 + (CX - 1) * (i // 8), pl.multiple_of((i % 8) * 8, 8))
            return carry

        lax.fori_loop(0, 16, edge, 0)
        if n < STEPS - 1:
            send_faces(F[(n + 1) % 2], all3, f_send.at[n + 1], f_recv.at[n + 1])

        def inner(i, carry):
            forward(n, 2 + i // 8, pl.multiple_of((i % 8) * 8, 8))
            return carry

        lax.fori_loop(0, (CX - 2) * 8, inner, 0)
        gather(n)
    wait_send(F[1], all3, f_send.at[STEPS - 1], f_recv.at[STEPS - 1])

    def allreduce(value, r):
        ebuf[r, 0] = value
        eslot_s[r, me_s] = value
        copies = []
        for d in range(1, n_shot):
            copies.append(
                pltpu.make_async_remote_copy(
                    src_ref=ebuf.at[r, 0],
                    dst_ref=eslot_s.at[r, me_s],
                    send_sem=e_send_s.at[r, d],
                    recv_sem=e_recv_s.at[r, d],
                    device_id=(lax.rem(me_s + d, n_shot), me_g),
                    device_id_type=MESH,
                )
            )
        for c in copies:
            c.start()
        for c in copies:
            c.wait_recv()
        total = eslot_s[r, 0]
        for d in range(1, n_shot):
            total = total + eslot_s[r, d]
        ebuf[r, 1] = total
        eslot_g[r, me_g] = total
        second = []
        for d in range(1, n_gx):
            second.append(
                pltpu.make_async_remote_copy(
                    src_ref=ebuf.at[r, 1],
                    dst_ref=eslot_g.at[r, me_g],
                    send_sem=e_send_g.at[r, d],
                    recv_sem=e_recv_g.at[r, d],
                    device_id=(me_s, lax.rem(me_g + d, n_gx)),
                    device_id_type=MESH,
                )
            )
        for c in second:
            c.start()
        for c in second:
            c.wait_recv()
        total = eslot_g[r, 0]
        for d in range(1, n_gx):
            total = total + eslot_g[r, d]
        for c in copies + second:
            c.wait_send()
        return jnp.sum(total)

    t = tr[...]
    energy = allreduce(t * t, 0)
    gn = jnp.full((8, HALF), grad_norm[0], f32)
    step = gn / (jnp.full((8, HALF), energy, f32) + tiny)
    for s in range(NS):
        r = residual[s] - step[0:STEPS] * t[s * STEPS : (s + 1) * STEPS]
        resid_o[s] = r
        amt[pl.ds(s * STEPS, STEPS), :] = r

    def adjoint(m, p, y8, force):
        now, nxt = U[(m + 1) % 2], U[m % 2]
        q = p - 1
        ys = pl.ds(y8, 8)
        ysp = pl.ds(pl.multiple_of(y8 + 8, 8), 8)
        n = STEPS - 1 - m
        pic = [None, None]
        for s in range(NS):
            if m > 0:
                mid, sums = neighbours(now, (s,), p, y8)
            for z in range(2):
                zs = pl.ds(z * HALF, HALF)
                u = inv[z, q, ys, :] * force[s, ys, zs]
                if m > 0:
                    u = u + ca[z, q, ys, :] * mid[z] + cc[z, q, ys, :] * sums[z]
                if m > 1:
                    u = u - cb[z, q, ys, :] * nxt[s, z, p, ysp, :]
                if m < STEPS - 1:
                    nxt[s, z, p, ysp, :] = u
                part = band[s, n, q, ys, zs] * u
                pic[z] = part if s == 0 else pic[z] + part
        for z in range(2):
            zs = pl.ds(z * HALF, HALF)
            if m == 0:
                img[q, ys, zs] = -pic[z]
            else:
                img[q, ys, zs] = img[q, ys, zs] - pic[z]

    force = rs

    def adjoint_plane(m, p):
        n = STEPS - 1 - m
        q = p - 1
        hot = rowhot[pl.ds(pl.multiple_of(q * NY, NY), NY), :]
        for s in range(NS):
            hi, lo = split2(amt[pl.ds(s * STEPS + n, 1), :])
            both = jnp.concatenate(
                [(hot * hi.astype(f32)).astype(bf16), (hot * lo.astype(f32)).astype(bf16)],
                axis=1,
            )
            force[s] = jnp.dot(both, zh2[...], preferred_element_type=f32)

        def chunk(i, carry):
            adjoint(m, p, pl.multiple_of(i * 8, 8), force)
            return carry

        lax.fori_loop(0, 8, chunk, 0)

    for m in range(STEPS):
        if m > 0:
            wait_recv(U[(m + 1) % 2], all2, u_send.at[m - 1], u_recv.at[m - 1])
        if m > 1:
            wait_send(U[m % 2], all2, u_send.at[m - 2], u_recv.at[m - 2])

        def edge(i, carry):
            adjoint_plane(m, 1 + (CX - 1) * i)
            return carry

        lax.fori_loop(0, 2, edge, 0)
        if m < STEPS - 1:
            send_faces(U[m % 2], all2, u_send.at[m], u_recv.at[m])

        def inner(i, carry):
            adjoint_plane(m, 2 + i)
            return carry

        lax.fori_loop(0, CX - 2, inner, 0)
    wait_send(U[0], all2, u_send.at[STEPS - 2], u_recv.at[STEPS - 2])

    scatter = []
    for d in range(1, n_shot):
        to = lax.rem(me_s + d, n_shot)
        scatter.append(
            pltpu.make_async_remote_copy(
                src_ref=img.at[to],
                dst_ref=rs.at[NS + d - 1],
                send_sem=g_send.at[0, d],
                recv_sem=g_recv.at[0, d],
                device_id=(to, me_g),
                device_id_type=MESH,
            )
        )
    for c in scatter:
        c.start()
    for c in scatter:
        c.wait_recv()

    def add(i, carry):
        ys = pl.ds(pl.multiple_of(i * 8, 8), 8)
        g = img[me_s, ys, :]
        for d in range(1, n_shot):
            g = g + rs[NS + d - 1, ys, :]
        grad_o[me_s, ys, :] = g
        g = g * g
        return carry + (g[:, :HALF] + g[:, HALF:])

    part = lax.fori_loop(0, 8, add, jnp.zeros((8, HALF), f32))
    spread = []
    for d in range(1, n_shot):
        to = lax.rem(me_s + d, n_shot)
        spread.append(
            pltpu.make_async_remote_copy(
                src_ref=grad_o.at[me_s],
                dst_ref=grad_o.at[me_s],
                send_sem=g_send.at[1, d],
                recv_sem=g_recv.at[1, d],
                device_id=(to, me_g),
                device_id_type=MESH,
            )
        )
    for c in spread:
        c.start()
    grad_energy = allreduce(part, 1)
    ratio = jnp.full((8, HALF), grad_energy, f32) / gn
    scal_o[pl.ds(0, 8), :] = step
    scal_o[pl.ds(8, 8), :] = ratio
    for d in range(1, n_shot):
        came = lax.rem(me_s + n_shot - d, n_shot)
        pltpu.make_async_remote_copy(
            src_ref=grad_o.at[came],
            dst_ref=grad_o.at[came],
            send_sem=g_send.at[1, d],
            recv_sem=g_recv.at[1, d],
            device_id=(came, me_g),
            device_id_type=MESH,
        ).wait_recv()
    for c in scatter + spread:
        c.wait_send()


def per_device(
    n_shot,
    n_gx,
    courant,
    absorb,
    model_image,
    direction,
    back_prev,
    back_now,
    scat_prev,
    scat_now,
    back_end,
    back_before_end,
    back_band,
    src_pos,
    wavelet,
    rec_pos,
    residual,
    grad_norm,
):
    hbm = pl.BlockSpec(memory_space=pl.ANY)
    vmem = pl.BlockSpec(memory_space=pltpu.VMEM)
    smem = pl.BlockSpec(memory_space=pltpu.SMEM)
    slab = (2, CX, NY, HALF)
    dma = pltpu.SemaphoreType.DMA
    gradient, residual_new, scal = pl.pallas_call(
        functools.partial(kernel, n_shot, n_gx),
        out_shape=(
            jax.ShapeDtypeStruct((CX, NY, NZ), f32),
            jax.ShapeDtypeStruct((NS, STEPS, REC), f32),
            jax.ShapeDtypeStruct((16, HALF), f32),
        ),
        in_specs=[hbm] * 9 + [smem] * 3 + [vmem] * 3,
        out_specs=(vmem, vmem, vmem),
        scratch_shapes=[
            pltpu.VMEM((3, NS, 2, CX + 2, PY, HALF), f32),
            pltpu.VMEM((3, NS, 2, CX + 2, PY, HALF), f32),
            pltpu.VMEM((NS, 2, CX + 2, PY, HALF), f32),
            pltpu.VMEM((NS, 2, CX + 2, PY, HALF), f32),
            pltpu.VMEM((NS, STEPS, CX, NY, NZ), f32),
            pltpu.VMEM(slab, f32),
            pltpu.VMEM(slab, f32),
            pltpu.VMEM(slab, f32),
            pltpu.VMEM(slab, f32),
            pltpu.VMEM(slab, f32),
            pltpu.VMEM(slab, f32),
            pltpu.VMEM((NS,) + slab, f32),
            pltpu.VMEM((CX * NY, REC), f32),
            pltpu.VMEM((NZ, REC), bf16),
            pltpu.VMEM((2 * REC, NZ), bf16),
            pltpu.VMEM((NS * STEPS, REC), f32),
            pltpu.VMEM((NS * STEPS, REC), f32),
            pltpu.VMEM((CX, NY, NZ), f32),
            pltpu.VMEM((NS + n_shot - 1, NY, NZ), f32),
            pltpu.VMEM((2, 2, 8, HALF), f32),
            pltpu.VMEM((2, n_shot, 8, HALF), f32),
            pltpu.VMEM((2, n_gx, 8, HALF), f32),
            dma((17,)),
            dma((STEPS, 2)),
            dma((STEPS, 2)),
            dma((STEPS - 1, 2)),
            dma((STEPS - 1, 2)),
            dma((2, n_shot)),
            dma((2, n_shot)),
            dma((2, n_gx)),
            dma((2, n_gx)),
            dma((2, n_shot)),
            dma((2, n_shot)),
        ],
        compiler_params=pltpu.CompilerParams(
            collective_id=0,
            has_side_effects=True,
            vmem_limit_bytes=52 * 1024 * 1024,
        ),
        name="lsrtm",
    )(
        courant,
        direction,
        back_prev,
        back_now,
        scat_prev,
        scat_now,
        back_end,
        back_before_end,
        back_band,
        absorb,
        wavelet,
        grad_norm,
        src_pos,
        rec_pos,
        residual,
    )
    step_size = scal[0, 0]
    ratio = scal[8, 0]
    return (
        model_image + step_size * direction,
        gradient + ratio * direction,
        residual_new,
    )


def solution(mesh):
    field = P("shot", "gx", None, None)
    grid = P("gx", None, None)
    in_specs = (
        grid,
        P(),
        grid,
        grid,
        field,
        field,
        field,
        field,
        field,
        field,
        P("shot", None, "gx", None, None),
        P("shot", None, None),
        P("shot", None),
        P("shot", "gx", None),
        P("shot", None, "gx"),
        P(),
    )
    return jax.shard_map(
        functools.partial(per_device, mesh.shape["shot"], mesh.shape["gx"]),
        mesh=mesh,
        in_specs=in_specs,
        out_specs=(grid, grid, P("shot", None, "gx")),
        check_vma=False,
    )
```

profile of v0, /device:TPU:1, one launch (start us, length us, event | category | flops | bytes accessed | tf_op | source)
XLA Modules:
  0.0 120.5 jit_solution(2441969878647615559)
XLA Ops:
  1.3 0.8 copy.19.src_pos
  2.1 0.8 copy.20.rec_pos
  2.9 0.0 copy-start
  2.9 1.0 copy-done
  3.9 0.0 copy-start.1
  3.9 1.0 copy-done.1
  5.0 0.0 copy-start.2
  5.0 0.7 copy-done.2
  5.7 0.0 copy-start.3
  5.7 0.7 copy-done.3
  6.3 0.0 copy-start.4
  6.3 0.7 copy-done.4
  7.0 0.0 copy-start.5
  7.0 110.0 %lsrtm.1 = (f32[8,64,256]{2,1,0:T(8,128)S(1)}, f32[2,4,128]{2,1,0:T(4,128)S(1)}, f32[16,128]{1,0:T(8,128)S(1)}) custom-call(f32[8,64,256]{2,1,0:T(8,128)S(1)} %copy-done.1, f32[8,64,256]{2,1,0:T(8,128)S(1)} %copy-done, f32[2,8,64,256]{3,2,1,0:T(8,128)} %back_prev_h.1, f32[2,8,64,256]{3,2,1,0:T(8,128)} %back_now_h.1, f32[2,8,64,256]{3,2,1,0:T(8,128)} %scat_prev_h.1, ...), custom_call_target="tpu_custom_call" | custom-call | tf_op jit(solution)/shard_map/lsrtm/pallas_call | solution.py:603
  117.0 0.6 fusion
  117.6 0.0 copy-done.5
  117.6 2.4 %multiply_add_fusion = (f32[8,64,256]{2,1,0:T(8,128)}, f32[8,64,256]{2,1,0:T(8,128)}) fusion(f32[8,64,256]{2,1,0:T(8,128)S(1)} %get-tuple-element.7, f32[8,64,256]{2,1,0:T(8,128)S(1)} %copy-done, f32[]{:T(128)} %bitcast.1, f32[8,64,256]{2,1,0:T(8,128)S(1)} %copy-done.5, f32[]{:T(128)} %bitcast), kind=kLoop, calls=%fused_computation | loop fusion | flops 524288 | bytes 2621448 | tf_op jit(solution)/shard_map/add | solution.py:674
  120.0 0.6 copy.23
Async XLA Ops:
  2.9 1.0 copy-start
  3.9 1.0 copy-start.1
  5.0 0.7 copy-start.2
  5.7 0.7 copy-start.3
  6.3 0.7 copy-start.4
  7.0 110.6 %copy-start.5 = (f32[8,64,256]{2,1,0:T(8,128)S(1)}, f32[8,64,256]{2,1,0:T(8,128)}, u32[]{:S(2)}) copy-start(f32[8,64,256]{2,1,0:T(8,128)} %param.18) | copy-start | bytes 1572868
where the time goes:
time: 121 us
  Pallas kernels  110 us (91%)
  local copies, waits for them, and re-layouts  6.88 us (6%)
  other arithmetic  2.4 us (2%)
  between operations  1.31 us (1%)
    pallas_call x1, Pallas kernels, per_device(): pl.pallas_call(functools.partial(kernel, n_shot, n_gx), out_shape=(jax.Sh...  110 us
    unnamed x15, local copies, waits for them, and re-layouts  6.29 us

commit v1 on v0

v1 whole, which is shorter than its diff:
```python
import functools

import jax
import jax.numpy as jnp
from jax import lax
from jax.experimental import pallas as pl
from jax.experimental.pallas import tpu as pltpu
from jax.sharding import PartitionSpec as P

damp_peak = 0.4
tiny = 1e-6
CX, NY, NZ = 8, 64, 256
NS, STEPS, REC, SRC = 2, 4, 128, 64
PY = 80
HU = 3
CU = CX + 2 * HU
HALF = 128
MESH = pl.DeviceIdType.MESH
f32 = jnp.float32
bf16 = jnp.bfloat16


def split2(v):
    hi = v.astype(bf16)
    lo = (v - hi.astype(f32)).astype(bf16)
    return hi, lo


def profile(pos, extent, low, high):
    gap = extent - 1 - pos
    low_f = low.astype(f32)
    high_f = high.astype(f32)
    near_low = jnp.where(pos < low, ((low - pos).astype(f32) / low_f) ** 2, 0.0)
    near_high = jnp.where(gap < high, ((high - gap).astype(f32) / high_f) ** 2, 0.0)
    return damp_peak * (near_low + near_high)


def kernel(
    n_shot,
    n_gx,
    courant_h,
    direction_h,
    back_prev_h,
    back_now_h,
    scat_prev_h,
    scat_now_h,
    back_end_h,
    back_before_h,
    band_h,
    absorb,
    wavelet,
    grad_norm,
    src_pos,
    rec_pos,
    residual,
    grad_o,
    resid_o,
    scal_o,
    F0,
    F1,
    R0,
    R1,
    U0,
    U1,
    band,
    c0,
    dirv,
    ca,
    cb,
    cc,
    inv,
    cnt,
    rowhot,
    zt,
    zh2,
    info,
    info_n,
    tr,
    tr_n,
    amt_s,
    img_r,
    img_t,
    rs,
    ebuf,
    eslot_s,
    eslot_g,
    ld_sem,
    f_send,
    f_recv,
    r_send,
    r_recv,
    h_send,
    h_recv,
    e_send_s,
    e_recv_s,
    e_send_g,
    e_recv_g,
    g_send,
    g_recv,
):
    me_s = lax.axis_index("shot")
    me_g = lax.axis_index("gx")
    has_left = me_g > 0
    has_right = me_g < n_gx - 1
    F = (F0, F1)
    R = (R0, R1)
    U = (U0, U1)
    own = pl.ds(HU, CX)
    data = pl.ds(8, NY)
    every = slice(None)

    loads = {}
    count_l = [0]

    def load(name, src, dst):
        c = pltpu.make_async_copy(src, dst, ld_sem.at[count_l[0]])
        count_l[0] += 1
        c.start()
        loads.setdefault(name, []).append(c)

    def wait_load(name):
        for c in loads[name]:
            c.wait()

    def load_field(name, src, dst):
        for z in range(2):
            load(name, src.at[:, :, :, pl.ds(z * HALF, HALF)], dst.at[:, z, pl.ds(1, CX), data, :])

    load_field("b0", back_now_h, F0.at[0])
    load_field("s0", scat_now_h, F0.at[1])
    load_field("r0", back_before_h, R0)
    for z in range(2):
        load("c", courant_h.at[:, :, pl.ds(z * HALF, HALF)], c0.at[z, own])
    load_field("bs1", back_prev_h, F1.at[0])
    load_field("bs1", scat_prev_h, F1.at[1])
    for z in range(2):
        load("bs1", direction_h.at[:, :, pl.ds(z * HALF, HALF)], dirv.at[z])
    load_field("r1", back_end_h, R1)
    load("r1", band_h, band)

    zero8 = jnp.zeros((8, HALF), f32)
    zero64 = jnp.zeros((NY, HALF), f32)
    lead_f = [(f, s, z) for f in range(2) for s in range(NS) for z in range(2)]
    lead_r = [(s, z) for s in range(NS) for z in range(2)]
    for p in (0, CX + 1):
        for b in range(2):
            for idx in lead_f:
                F[b][idx + (p, data, every)] = zero64
            for idx in lead_r:
                R[b][idx + (p, data, every)] = zero64
    for z in range(2):
        for p in range(HU):
            c0[z, p] = zero64
            c0[z, HU + CX + p] = zero64
    for g in range(2):
        info_n[g, pl.ds(0, 8), :] = zero8
        info_n[g, pl.ds(8, 8), :] = zero8
        tr_n[g] = zero8

    bar = pltpu.get_barrier_semaphore()
    for d in range(1, n_gx):
        pl.semaphore_signal(
            bar, inc=1, device_id=(me_s, lax.rem(me_g + d, n_gx)), device_id_type=MESH
        )
    for d in range(1, n_shot):
        pl.semaphore_signal(
            bar, inc=1, device_id=(lax.rem(me_s + d, n_shot), me_g), device_id_type=MESH
        )

    rec_row = (rec_pos[0, 0:1, :] * NY + rec_pos[1, 0:1, :]).astype(f32)
    rec_z = rec_pos[2, 0:1, :].astype(f32)
    for s in range(NS):
        info[pl.ds(s * STEPS, STEPS), :] = residual[s]
    info[pl.ds(8, 1), :] = rec_row
    info[pl.ds(9, 1), :] = rec_z
    info[pl.ds(10, 6), :] = jnp.zeros((6, REC), f32)

    class Pair:
        def __init__(self, to_left, to_right, send, recv):
            self.refs = (to_left, to_right)
            self.send = send
            self.recv = recv

        def copy(self, side):
            src, dst = self.refs[side]
            return pltpu.make_async_remote_copy(
                src_ref=src,
                dst_ref=dst,
                send_sem=self.send.at[side],
                recv_sem=self.recv.at[side],
                device_id=(me_s, me_g - 1 if side == 0 else me_g + 1),
                device_id_type=MESH,
            )

        def start(self):
            @pl.when(has_left)
            def _():
                self.copy(0).start()

            @pl.when(has_right)
            def _():
                self.copy(1).start()

        def wait_recv(self):
            @pl.when(has_right)
            def _():
                self.copy(0).wait_recv()

            @pl.when(has_left)
            def _():
                self.copy(1).wait_recv()

        def wait_send(self):
            @pl.when(has_left)
            def _():
                self.copy(0).wait_send()

            @pl.when(has_right)
            def _():
                self.copy(1).wait_send()

    def face(buf, lead, p):
        return buf.at[(every,) * lead + (p, data, every)]

    def bs_faces(n):
        b = F[n % 2]
        return Pair(
            (face(b, 3, 1), face(b, 3, CX + 1)),
            (face(b, 3, CX), face(b, 3, 0)),
            f_send.at[n],
            f_recv.at[n],
        )

    def r_faces(n):
        b = R[n % 2]
        return Pair(
            (face(b, 2, 1), face(b, 2, CX + 1)),
            (face(b, 2, CX), face(b, 2, 0)),
            r_send.at[n],
            r_recv.at[n],
        )

    c_halo = Pair(
        (c0.at[:, pl.ds(HU, HU)], c0.at[:, pl.ds(HU + CX, HU)]),
        (c0.at[:, pl.ds(CX, HU)], c0.at[:, pl.ds(0, HU)]),
        h_send.at[0],
        h_recv.at[0],
    )
    info_halo = Pair((info, info_n.at[1]), (info, info_n.at[0]), h_send.at[1], h_recv.at[1])
    tr_halo = Pair((tr, tr_n.at[1]), (tr, tr_n.at[0]), h_send.at[2], h_recv.at[2])

    pl.semaphore_wait(bar, n_gx - 1 + n_shot - 1)
    wait_load("b0")
    wait_load("s0")
    bs_faces(0).start()
    wait_load("r0")
    r_faces(0).start()
    info_halo.start()
    wait_load("c")
    c_halo.start()

    def pads(p, carry):
        for b in range(2):
            for idx in lead_f:
                F[b][idx + (p, pl.ds(0, 8), every)] = zero8
                F[b][idx + (p, pl.ds(72, 8), every)] = zero8
            for idx in lead_r:
                R[b][idx + (p, pl.ds(0, 8), every)] = zero8
                R[b][idx + (p, pl.ds(72, 8), every)] = zero8
        return carry

    lax.fori_loop(0, CX + 2, pads, 0)

    def pads_u(p, carry):
        for b in range(2):
            for idx in lead_r:
                U[b][idx + (p, pl.ds(0, 8), every)] = zero8
                U[b][idx + (p, pl.ds(72, 8), every)] = zero8
        return carry

    lax.fori_loop(0, CU, pads_u, 0)

    def to_col(row, n):
        eye = lax.broadcasted_iota(jnp.int32, (n, n), 0) == lax.broadcasted_iota(
            jnp.int32, (n, n), 1
        )
        return jnp.sum(jnp.where(eye, row, 0.0), axis=1, keepdims=True)

    first_row = ((me_g * CX - HU) * NY).astype(f32)

    def hot_rows(row, lo, n):
        rows = lax.broadcasted_iota(jnp.int32, (n, REC), 0).astype(f32) + (first_row + lo)
        rowhot[pl.ds(lo, n), :] = jnp.where(rows == row, 1.0, 0.0).astype(bf16)

    lane_z = lax.broadcasted_iota(jnp.int32, (REC, NZ), 1).astype(f32)

    def hot_z(z_row, g):
        hot = jnp.where(lane_z == to_col(z_row, REC), 1.0, 0.0).astype(bf16)
        zh2[g, pl.ds(0, REC), :] = hot
        zh2[g, pl.ds(REC, REC), :] = hot

    hot_rows(rec_row, HU * NY, CX * NY)
    hot_z(rec_z, 1)
    zt[...] = jnp.where(
        lax.broadcasted_iota(jnp.int32, (NZ, REC), 0).astype(f32) == rec_z, 1.0, 0.0
    ).astype(bf16)

    nx = n_gx * CX
    lane = lax.broadcasted_iota(jnp.int32, (8, HALF), 1)
    sub = lax.broadcasted_iota(jnp.int32, (8, HALF), 0)
    damp_z = [profile(lane + z * HALF, NZ, absorb[4], absorb[5]) for z in range(2)]

    def coef(i, carry):
        pos_x = jnp.full((8, HALF), me_g * CX - HU + i, jnp.int32)
        damp_x = profile(pos_x, nx, absorb[0], absorb[1])
        for y in range(8):
            ys = pl.ds(y * 8, 8)
            damp_xy = damp_x + profile(sub + y * 8, NY, absorb[2], absorb[3])
            for z in range(2):
                damping = damp_xy + damp_z[z]
                c = c0[z, i, ys, :]
                iv = 1.0 / (1.0 + damping)
                inv[z, i, ys, :] = iv
                ca[z, i, ys, :] = (2.0 - 6.0 * c) * iv
                cb[z, i, ys, :] = (1.0 - damping) * iv
                cc[z, i, ys, :] = c * iv
        return carry

    lax.fori_loop(HU, HU + CX, coef, 0)

    src_hot = []
    for s in range(NS):
        s_row = ((src_pos[0, s : s + 1, :] - me_g * CX) * NY + src_pos[1, s : s + 1, :]).astype(
            f32
        )
        s_z = to_col(src_pos[2, s : s + 1, :].astype(f32), SRC)
        s_hot = jnp.where(
            lax.broadcasted_iota(jnp.int32, (SRC, NZ), 1).astype(f32) == s_z, 1.0, 0.0
        ).astype(bf16)
        src_hot.append((s_row, s_hot))

    def count(p, carry):
        rows = (lax.broadcasted_iota(jnp.int32, (NY, SRC), 0) + p * NY).astype(f32)
        for s in range(NS):
            hot = jnp.where(rows == src_hot[s][0], 1.0, 0.0).astype(bf16)
            n = jnp.dot(hot, src_hot[s][1], preferred_element_type=f32)
            for z in range(2):
                cnt[s, z, p] = n[:, z * HALF : (z + 1) * HALF] * inv[z, HU + p]
        return carry

    lax.fori_loop(0, CX, count, 0, unroll=2)

    first = lane == 0
    last = lane == HALF - 1

    def neighbours(ref, lead, p, y8):
        ys = pl.ds(8 + y8, 8)
        mid = [ref[lead + (z, p, ys, every)] for z in range(2)]
        right = [pltpu.roll(m, 1, 1) for m in mid]
        left = [pltpu.roll(m, HALF - 1, 1) for m in mid]
        low = [jnp.where(first, 0.0, right[0]), jnp.where(first, right[0], right[1])]
        high = [jnp.where(last, left[1], left[0]), jnp.where(last, 0.0, left[1])]
        sums = []
        for z in range(2):
            t = ref[lead + (z, p + 1, ys, every)] + ref[lead + (z, p - 1, ys, every)]
            t = t + (
                ref[lead + (z, p, pl.ds(y8 + 9, 8), every)]
                + ref[lead + (z, p, pl.ds(y8 + 7, 8), every)]
            )
            sums.append(t + (low[z] + high[z]))
        return mid, sums

    def step_bs(n, p):
        now, nxt = F[n % 2], F[(n + 1) % 2]
        q = p - 1
        i = q + HU

        def chunk(j, carry):
            y8 = pl.multiple_of(j * 8, 8)
            ys = pl.ds(y8, 8)
            ysp = pl.ds(pl.multiple_of(y8 + 8, 8), 8)
            a = [ca[z, i, ys, :] for z in range(2)]
            b = [cb[z, i, ys, :] for z in range(2)]
            c = [cc[z, i, ys, :] for z in range(2)]
            di = [dirv[z, q, ys, :] for z in range(2)]
            for s in range(NS):
                w = wavelet[s, n]
                mid, sums = neighbours(now, (0, s), p, y8)
                acc = []
                for z in range(2):
                    old = nxt[0, s, z, p, ysp, :]
                    new = (
                        a[z] * mid[z]
                        - b[z] * old
                        + c[z] * sums[z]
                        + w * cnt[s, z, q, ys, :]
                    )
                    nxt[0, s, z, p, ysp, :] = new
                    acc.append((new - mid[z]) - (mid[z] - old))
                mid, sums = neighbours(now, (1, s), p, y8)
                for z in range(2):
                    old = nxt[1, s, z, p, ysp, :]
                    nxt[1, s, z, p, ysp, :] = (
                        a[z] * mid[z] - b[z] * old + c[z] * (sums[z] - di[z] * acc[z])
                    )
            return carry

        lax.fori_loop(0, 8, chunk, 0, unroll=8)

    def step_r(n, p):
        now, nxt = R[n % 2], R[(n + 1) % 2]
        q = p - 1
        i = q + HU
        m = STEPS - 1 - n

        def chunk(j, carry):
            y8 = pl.multiple_of(j * 8, 8)
            ys = pl.ds(y8, 8)
            ysp = pl.ds(pl.multiple_of(y8 + 8, 8), 8)
            a = [ca[z, i, ys, :] for z in range(2)]
            c = [cc[z, i, ys, :] for z in range(2)]
            layer = [cb[z, i, ys, :] < 1.0 for z in range(2)]
            for s in range(NS):
                w = wavelet[s, m]
                mid, sums = neighbours(now, (s,), p, y8)
                for z in range(2):
                    zs = pl.ds(z * HALF, HALF)
                    old = nxt[s, z, p, ysp, :]
                    new = a[z] * mid[z] - old + c[z] * sums[z] + w * cnt[s, z, q, ys, :]
                    new = jnp.where(layer[z], band[s, m, q, ys, zs], new)
                    nxt[s, z, p, ysp, :] = new
                    band[s, m, q, ys, zs] = (new - mid[z]) - (mid[z] - old)
            return carry

        lax.fori_loop(0, 8, chunk, 0, unroll=8)

    def gather(n):
        ref = F[(n + 1) % 2]
        zero = jnp.zeros((NY, REC), f32)

        def one(p, carry):
            hot = rowhot[pl.ds(pl.multiple_of((p + HU) * NY, NY), NY), :].astype(f32)
            parts = []
            for s in range(NS):
                v = jnp.concatenate([ref[1, s, z, p + 1, data, :] for z in range(2)], axis=1)
                parts.extend(split2(v))
            g = jnp.dot(jnp.concatenate(parts, axis=0), zt[...], preferred_element_type=f32)
            return tuple(
                carry[s] + hot * (g[2 * s * NY : (2 * s + 1) * NY] + g[(2 * s + 1) * NY : (2 * s + 2) * NY])
                for s in range(NS)
            )

        got = lax.fori_loop(0, CX, one, (zero, zero), unroll=4)
        for s in range(NS):
            tr[pl.ds(s * STEPS + n, 1), :] = jnp.sum(got[s], axis=0, keepdims=True)

    def inject(m, amounts, lo, hi):
        nxt = U[m % 2]
        n = STEPS - 1 - m

        def plane(i, carry):
            g = (i + CX - HU) // CX
            hot = rowhot[pl.ds(pl.multiple_of(i * NY, NY), NY), :].astype(f32)
            parts = []
            for s in range(NS):
                v = amounts[g, pl.ds(s * STEPS + n, 1), :]
                v_hi = v.astype(bf16).astype(f32)
                parts.append(
                    jnp.concatenate(
                        [(hot * v_hi).astype(bf16), (hot * (v - v_hi)).astype(bf16)], axis=1
                    )
                )
            e = jnp.dot(jnp.concatenate(parts, axis=0), zh2[g], preferred_element_type=f32)
            for s in range(NS):
                for z in range(2):
                    u = inv[z, i] * e[s * NY : (s + 1) * NY, z * HALF : (z + 1) * HALF]
                    if m > 1:
                        u = u - cb[z, i] * nxt[s, z, i, data, :]
                    nxt[s, z, i, data, :] = u
            return carry

        lax.fori_loop(lo, hi, plane, 0, unroll=2)

    def level(m, img):
        now, nxt = U[(m + 1) % 2], U[m % 2]
        n = STEPS - 1 - m

        def plane(image, i, carry):
            q = i - HU

            def chunk(j, inner):
                y8 = pl.multiple_of(j * 8, 8)
                ys = pl.ds(y8, 8)
                ysp = pl.ds(pl.multiple_of(y8 + 8, 8), 8)
                pic = [None, None]
                for s in range(NS):
                    if m > 0:
                        mid, sums = neighbours(now, (s,), i, y8)
                    for z in range(2):
                        u = nxt[s, z, i, ysp, :]
                        if m > 0:
                            u = u + ca[z, i, ys, :] * mid[z] + cc[z, i, ys, :] * sums[z]
                            if m < STEPS - 1:
                                nxt[s, z, i, ysp, :] = u
                        if image:
                            part = band[s, n, q, ys, pl.ds(z * HALF, HALF)] * u
                            pic[z] = part if s == 0 else pic[z] + part
                if image:
                    for z in range(2):
                        zs = pl.ds(z * HALF, HALF)
                        old = 0.0 if m == 0 else img[q, ys, zs]
                        img[q, ys, zs] = old + pic[z]
                return inner

            lax.fori_loop(0, 8, chunk, 0, unroll=8)
            return carry

        if 0 < m < STEPS - 1:
            lax.fori_loop(m, HU, functools.partial(plane, False), 0)
            lax.fori_loop(HU + CX, CU - m, functools.partial(plane, False), 0)
        lax.fori_loop(HU, HU + CX, functools.partial(plane, True), 0)

    for n in range(STEPS):
        bs_faces(n).wait_recv()
        if n == 0:
            wait_load("bs1")
        if n > 0:
            bs_faces(n - 1).wait_send()

        def edge_bs(k, carry):
            step_bs(n, 1 + (CX - 1) * k)
            return carry

        lax.fori_loop(0, 2, edge_bs, 0)
        if n < STEPS - 1:
            bs_faces(n + 1).start()
        r_faces(n).wait_recv()
        if n == 0:
            wait_load("r1")
        if n > 0:
            r_faces(n - 1).wait_send()

        def edge_r(k, carry):
            step_r(n, 1 + (CX - 1) * k)
            return carry

        lax.fori_loop(0, 2, edge_r, 0)
        if n < STEPS - 1:
            r_faces(n + 1).start()

        def inner_bs(p, carry):
            step_bs(n, p)
            return carry

        lax.fori_loop(2, CX, inner_bs, 0)

        def inner_r(p, carry):
            step_r(n, p)
            return carry

        lax.fori_loop(2, CX, inner_r, 0)
        gather(n)
        if n == 0:
            info_halo.wait_recv()
            c_halo.wait_recv()
            for g, lo in ((0, 0), (1, (HU + CX) * NY)):
                hot_rows(info_n[g, pl.ds(8, 1), :], lo, HU * NY)
                hot_z(info_n[g, pl.ds(9, 1), :], 2 * g)
            lax.fori_loop(0, HU, coef, 0)
            lax.fori_loop(HU + CX, CU, coef, 0)
            amt_s[0, 0] = info_n[0, pl.ds(0, 8), :]
            amt_s[0, 1] = info[pl.ds(0, 8), :]
            amt_s[0, 2] = info_n[1, pl.ds(0, 8), :]
        inject(n, amt_s.at[0], n, CU - n)
        level(n, img_r)
    bs_faces(STEPS - 1).wait_send()
    r_faces(STEPS - 1).wait_send()
    info_halo.wait_send()
    c_halo.wait_send()

    def to_shots(r):
        return [
            pltpu.make_async_remote_copy(
                src_ref=ebuf.at[r, 0],
                dst_ref=eslot_s.at[r, me_s],
                send_sem=e_send_s.at[r, d],
                recv_sem=e_recv_s.at[r, d],
                device_id=(lax.rem(me_s + d, n_shot), me_g),
                device_id_type=MESH,
            )
            for d in range(1, n_shot)
        ]

    def to_slabs(r):
        return [
            pltpu.make_async_remote_copy(
                src_ref=ebuf.at[r, 1],
                dst_ref=eslot_g.at[r, me_g],
                send_sem=e_send_g.at[r, d],
                recv_sem=e_recv_g.at[r, d],
                device_id=(me_s, lax.rem(me_g + d, n_gx)),
                device_id_type=MESH,
            )
            for d in range(1, n_gx)
        ]

    def sum_start(value, r):
        ebuf[r, 0] = value
        eslot_s[r, me_s] = value
        for c in to_shots(r):
            c.start()

    def sum_middle(r):
        for c in to_shots(r):
            c.wait_recv()
        total = eslot_s[r, 0]
        for d in range(1, n_shot):
            total = total + eslot_s[r, d]
        ebuf[r, 1] = total
        eslot_g[r, me_g] = total
        for c in to_slabs(r):
            c.start()

    def sum_end(r):
        for c in to_slabs(r):
            c.wait_recv()
        total = eslot_g[r, 0]
        for d in range(1, n_gx):
            total = total + eslot_g[r, d]
        return jnp.sum(total)

    t = tr[...]
    tr_halo.start()
    sum_start(t * t, 0)
    amt_s[1, 1] = t
    inject(0, amt_s.at[1], HU, HU + CX)
    tr_halo.wait_recv()
    amt_s[1, 0] = tr_n[0]
    amt_s[1, 2] = tr_n[1]
    inject(0, amt_s.at[1], 0, HU)
    inject(0, amt_s.at[1], HU + CX, CU)
    level(0, img_t)
    sum_middle(0)
    for m in range(1, STEPS):
        inject(m, amt_s.at[1], m, CU - m)
        level(m, img_t)
    energy = sum_end(0)
    gn = jnp.full((8, HALF), grad_norm[0], f32)
    step = gn / (jnp.full((8, HALF), energy, f32) + tiny)
    for s in range(NS):
        resid_o[s] = residual[s] - step[0:STEPS] * t[s * STEPS : (s + 1) * STEPS]

    def combine(q):
        for y in range(8):
            ys = pl.ds(y * 8, 8)
            for z in range(2):
                zs = pl.ds(z * HALF, HALF)
                img_r[q, ys, zs] = c0[z, HU + q, ys, :] * (
                    step * img_t[q, ys, zs] - img_r[q, ys, zs]
                )

    scatter = []
    for d in range(1, n_shot):
        to = lax.rem(me_s + d, n_shot)
        combine(to)
        c = pltpu.make_async_remote_copy(
            src_ref=img_r.at[to],
            dst_ref=rs.at[d - 1],
            send_sem=g_send.at[0, d],
            recv_sem=g_recv.at[0, d],
            device_id=(to, me_g),
            device_id_type=MESH,
        )
        c.start()
        scatter.append(c)
    combine(me_s)
    for c in scatter:
        c.wait_recv()

    def add(i, carry):
        ys = pl.ds(pl.multiple_of(i * 8, 8), 8)
        g = img_r[me_s, ys, :]
        for d in range(1, n_shot):
            g = g + rs[d - 1, ys, :]
        grad_o[me_s, ys, :] = g
        g = g * g
        return carry + (g[:, :HALF] + g[:, HALF:])

    part = lax.fori_loop(0, 8, add, jnp.zeros((8, HALF), f32), unroll=8)
    sum_start(part, 1)
    spread = []
    for d in range(1, n_shot):
        to = lax.rem(me_s + d, n_shot)
        c = pltpu.make_async_remote_copy(
            src_ref=grad_o.at[me_s],
            dst_ref=grad_o.at[me_s],
            send_sem=g_send.at[1, d],
            recv_sem=g_recv.at[1, d],
            device_id=(to, me_g),
            device_id_type=MESH,
        )
        c.start()
        spread.append(c)
    sum_middle(1)
    grad_energy = sum_end(1)
    ratio = jnp.full((8, HALF), grad_energy, f32) / gn
    scal_o[pl.ds(0, 8), :] = step
    scal_o[pl.ds(8, 8), :] = ratio
    for d in range(1, n_shot):
        came = lax.rem(me_s + n_shot - d, n_shot)
        pltpu.make_async_remote_copy(
            src_ref=grad_o.at[came],
            dst_ref=grad_o.at[came],
            send_sem=g_send.at[1, d],
            recv_sem=g_recv.at[1, d],
            device_id=(came, me_g),
            device_id_type=MESH,
        ).wait_recv()
    tr_halo.wait_send()
    for r in range(2):
        for c in to_shots(r) + to_slabs(r):
            c.wait_send()
    for c in scatter + spread:
        c.wait_send()


def finish(scal, gradient, direction, model_image, resid, image_o, dir_o, resid_o):
    step = scal[0:1, 0:1]
    ratio = scal[8:9, 0:1]

    def plane(p, carry):
        d = direction[p]
        image_o[p] = model_image[p] + step * d
        dir_o[p] = gradient[p] + ratio * d
        return carry

    lax.fori_loop(0, CX, plane, 0)
    resid_o[...] = resid[...]


def per_device(
    n_shot,
    n_gx,
    courant,
    absorb,
    model_image,
    direction,
    back_prev,
    back_now,
    scat_prev,
    scat_now,
    back_end,
    back_before_end,
    back_band,
    src_pos,
    wavelet,
    rec_pos,
    residual,
    grad_norm,
):
    hbm = pl.BlockSpec(memory_space=pl.ANY)
    vmem = pl.BlockSpec(memory_space=pltpu.VMEM)
    smem = pl.BlockSpec(memory_space=pltpu.SMEM)
    slab = (2, CX, NY, HALF)
    wide = (2, CU, NY, HALF)
    dma = pltpu.SemaphoreType.DMA
    V = pltpu.VMEM
    gradient, resid, scal = pl.pallas_call(
        functools.partial(kernel, n_shot, n_gx),
        out_shape=(
            jax.ShapeDtypeStruct((CX, NY, NZ), f32),
            jax.ShapeDtypeStruct((NS, STEPS, REC), f32),
            jax.ShapeDtypeStruct((16, HALF), f32),
        ),
        in_specs=[hbm] * 9 + [smem] * 3 + [vmem] * 3,
        out_specs=(vmem, vmem, vmem),
        scratch_shapes=[
            V((2, NS, 2, CX + 2, PY, HALF), f32),
            V((2, NS, 2, CX + 2, PY, HALF), f32),
            V((NS, 2, CX + 2, PY, HALF), f32),
            V((NS, 2, CX + 2, PY, HALF), f32),
            V((NS, 2, CU, PY, HALF), f32),
            V((NS, 2, CU, PY, HALF), f32),
            V((NS, STEPS, CX, NY, NZ), f32),
            V(wide, f32),
            V(slab, f32),
            V(wide, f32),
            V(wide, f32),
            V(wide, f32),
            V(wide, f32),
            V((NS,) + slab, f32),
            V((CU * NY, REC), bf16),
            V((NZ, REC), bf16),
            V((3, 2 * REC, NZ), bf16),
            V((16, REC), f32),
            V((2, 16, REC), f32),
            V((NS * STEPS, REC), f32),
            V((2, NS * STEPS, REC), f32),
            V((2, 3, NS * STEPS, REC), f32),
            V((CX, NY, NZ), f32),
            V((CX, NY, NZ), f32),
            V((n_shot - 1, NY, NZ), f32),
            V((2, 2, 8, HALF), f32),
            V((2, n_shot, 8, HALF), f32),
            V((2, n_gx, 8, HALF), f32),
            dma((17,)),
            dma((STEPS, 2)),
            dma((STEPS, 2)),
            dma((STEPS, 2)),
            dma((STEPS, 2)),
            dma((3, 2)),
            dma((3, 2)),
            dma((2, n_shot)),
            dma((2, n_shot)),
            dma((2, n_gx)),
            dma((2, n_gx)),
            dma((2, n_shot)),
            dma((2, n_shot)),
        ],
        compiler_params=pltpu.CompilerParams(
            collective_id=0,
            has_side_effects=True,
            vmem_limit_bytes=58 * 1024 * 1024,
        ),
        name="lsrtm",
    )(
        courant,
        direction,
        back_prev,
        back_now,
        scat_prev,
        scat_now,
        back_end,
        back_before_end,
        back_band,
        absorb,
        wavelet,
        grad_norm,
        jnp.transpose(src_pos, (2, 0, 1)),
        jnp.transpose(rec_pos, (2, 0, 1)),
        residual,
    )
    return pl.pallas_call(
        finish,
        out_shape=(
            jax.ShapeDtypeStruct((CX, NY, NZ), f32),
            jax.ShapeDtypeStruct((CX, NY, NZ), f32),
            jax.ShapeDtypeStruct((NS, STEPS, REC), f32),
        ),
        in_specs=[vmem] * 5,
        out_specs=(vmem, vmem, vmem),
        compiler_params=pltpu.CompilerParams(vmem_limit_bytes=16 * 1024 * 1024),
        name="finish",
    )(scal, gradient, direction, model_image, resid)


def solution(mesh):
    field = P("shot", "gx", None, None)
    grid = P("gx", None, None)
    in_specs = (
        grid,
        P(),
        grid,
        grid,
        field,
        field,
        field,
        field,
        field,
        field,
        P("shot", None, "gx", None, None),
        P("shot", None, None),
        P("shot", None),
        P("shot", "gx", None),
        P("shot", None, "gx"),
        P(),
    )
    return jax.shard_map(
        functools.partial(per_device, mesh.shape["shot"], mesh.shape["gx"]),
        mesh=mesh,
        in_specs=in_specs,
        out_specs=(grid, grid, P("shot", None, "gx")),
        check_vma=False,
    )
```

time: 121 us -> 80.2 us (0.66)
  Pallas kernels: 110 us -> 75.7 us
  local copies, waits for them, and re-layouts: 6.88 us -> 2.41 us
  other arithmetic: 2.4 us -> 0 us
    pallas_call x1, Pallas kernels: 110 us -> 74.4 us  [per_device(): pl.pallas_call(functools.partial(kernel, n_shot, n_gx), out_shape=(jax.Sh...]
    unnamed x15 -> x10, local copies, waits for them, and re-layouts: 6.29 us -> 2.41 us
    add x1 -> x0, other arithmetic: 2.4 us -> none  [per_device(): gradient + ratio * direction]
    pallas_call x0 -> x1, Pallas kernels: none -> 1.34 us  [per_device(): pl.pallas_call(finish, out_shape=(jax.ShapeDtypeStruct((CX, NY, NZ), f32)...]
where the time goes in v1:
time: 80.2 us; the launch traced here: 79.4 us
  Pallas kernels  75.7 us (94%)
  local copies, waits for them, and re-layouts  2.41 us (3%)
  between operations  1.33 us (2%)
    pallas_call x1, Pallas kernels, per_device(): pl.pallas_call(functools.partial(kernel, n_shot, n_gx), out_shape=(jax.Sh...  74.4 us
    unnamed x10, local copies, waits for them, and re-layouts  2.41 us

profile of v1, /device:TPU:1, one launch (start us, length us, event | category | flops | bytes accessed | tf_op | source)
XLA Modules:
  0.0 79.4 jit_solution(1704325055860402841)
XLA Ops:
  1.3 0.0 copy-start
  1.3 0.0 copy-start.1
  1.3 74.4 %lsrtm.1 = (f32[8,64,256]{2,1,0:T(8,128)}, f32[2,4,128]{2,1,0:T(4,128)}, f32[16,128]{1,0:T(8,128)}) custom-call(f32[8,64,256]{2,1,0:T(8,128)} %courant_h.1, f32[8,64,256]{2,1,0:T(8,128)} %direction.1, f32[2,8,64,256]{3,2,1,0:T(8,128)} %back_prev_h.1, f32[2,8,64,256]{3,2,1,0:T(8,128)} %back_now_h.1, f32[2,8,64,256]{3,2,1,0:T(8,128)} %scat_prev_h.1, ...), custom_call_target="tpu_custom_call" | custom-call | tf_op jit(solution)/shard_map/lsrtm/pallas_call | solution.py:768
  75.7 0.0 copy-done
  75.7 0.0 copy-done.1
  75.7 0.0 copy-start.2
  75.7 1.0 %copy-done.2 = f32[8,64,256]{2,1,0:T(8,128)S(1)} copy-done((f32[8,64,256]{2,1,0:T(8,128)S(1)}, f32[8,64,256]{2,1,0:T(8,128)}, u32[]{:S(2)}) %copy-start.2) | copy-done | bytes 524312
  76.7 0.0 copy-start.3
  76.7 0.7 copy-done.3
  77.4 0.0 copy-start.4
  77.4 0.7 copy-done.4
  78.1 1.3 %finish.1 = (f32[8,64,256]{2,1,0:T(8,128)}, f32[8,64,256]{2,1,0:T(8,128)}, f32[2,4,128]{2,1,0:T(4,128)}) custom-call(f32[16,128]{1,0:T(8,128)S(1)} %copy-done.3, f32[8,64,256]{2,1,0:T(8,128)S(1)} %copy-done.2, f32[8,64,256]{2,1,0:T(8,128)S(1)} %copy-done, f32[8,64,256]{2,1,0:T(8,128)S(1)} %copy-done.1, f32[2,4,128]{2,1,0:T(4,128)S(1)} %copy-done.4), custom_call_target="tpu_custom_call" | custom-call | tf_op jit(solution)/shard_map/finish/pallas_call | solution.py:843
Async XLA Ops:
  1.3 74.4 %copy-start = (f32[8,64,256]{2,1,0:T(8,128)S(1)}, f32[8,64,256]{2,1,0:T(8,128)}, u32[]{:S(2)}) copy-start(f32[8,64,256]{2,1,0:T(8,128)} %direction.1) | copy-start | bytes 1572868
  1.3 74.4 %copy-start.1 = (f32[8,64,256]{2,1,0:T(8,128)S(1)}, f32[8,64,256]{2,1,0:T(8,128)}, u32[]{:S(2)}) copy-start(f32[8,64,256]{2,1,0:T(8,128)} %model_image.1) | copy-start | bytes 1572868
  75.7 1.0 %copy-start.2 = (f32[8,64,256]{2,1,0:T(8,128)S(1)}, f32[8,64,256]{2,1,0:T(8,128)}, u32[]{:S(2)}) copy-start(f32[8,64,256]{2,1,0:T(8,128)} %get-tuple-element.7.gradient) | copy-start | bytes 1572868
  76.7 0.7 copy-start.3
  77.4 0.7 copy-start.4

commit v2 on v1

--- a/solution.py
+++ b/solution.py
@@ -78,6 +78,7 @@
     tr,
     tr_n,
     amt_s,
+    E,
     img_r,
     img_t,
     rs,
@@ -249,6 +250,52 @@
     info_halo = Pair((info, info_n.at[1]), (info, info_n.at[0]), h_send.at[1], h_recv.at[1])
     tr_halo = Pair((tr, tr_n.at[1]), (tr, tr_n.at[0]), h_send.at[2], h_recv.at[2])
 
+    def pads(p, carry):
+        for b in range(2):
+            for idx in lead_f:
+                F[b][idx + (p, pl.ds(0, 8), every)] = zero8
+                F[b][idx + (p, pl.ds(72, 8), every)] = zero8
+            for idx in lead_r:
+                R[b][idx + (p, pl.ds(0, 8), every)] = zero8
+                R[b][idx + (p, pl.ds(72, 8), every)] = zero8
+        return carry
+
+    lax.fori_loop(0, CX + 2, pads, 0)
+
+    def pads_u(p, carry):
+        for b in range(2):
+            for idx in lead_r:
+                U[b][idx + (p, pl.ds(0, 8), every)] = zero8
+                U[b][idx + (p, pl.ds(72, 8), every)] = zero8
+        return carry
+
+    lax.fori_loop(0, CU, pads_u, 0)
+
+    def to_col(row, n):
+        eye = lax.broadcasted_iota(jnp.int32, (n, n), 0) == lax.broadcasted_iota(
+            jnp.int32, (n, n), 1
+        )
+        return jnp.sum(jnp.where(eye, row, 0.0), axis=1, keepdims=True)
+
+    first_row = ((me_g * CX - HU) * NY).astype(f32)
+
+    def hot_rows(row, lo, n):
+        rows = lax.broadcasted_iota(jnp.int32, (n, REC), 0).astype(f32) + (first_row + lo)
+        rowhot[pl.ds(lo, n), :] = jnp.where(rows == row, 1.0, 0.0).astype(bf16)
+
+    lane_z = lax.broadcasted_iota(jnp.int32, (REC, NZ), 1).astype(f32)
+
+    def hot_z(z_row, g):
+        hot = jnp.where(lane_z == to_col(z_row, REC), 1.0, 0.0).astype(bf16)
+        zh2[g, pl.ds(0, REC), :] = hot
+        zh2[g, pl.ds(REC, REC), :] = hot
+
+    hot_rows(rec_row, HU * NY, CX * NY)
+    hot_z(rec_z, 1)
+    zt[...] = jnp.where(
+        lax.broadcasted_iota(jnp.int32, (NZ, REC), 0).astype(f32) == rec_z, 1.0, 0.0
+    ).astype(bf16)
+
     pl.semaphore_wait(bar, n_gx - 1 + n_shot - 1)
     wait_load("b0")
     wait_load("s0")
@@ -258,52 +305,6 @@
     info_halo.start()
     wait_load("c")
     c_halo.start()
-
-    def pads(p, carry):
-        for b in range(2):
-            for idx in lead_f:
-                F[b][idx + (p, pl.ds(0, 8), every)] = zero8
-                F[b][idx + (p, pl.ds(72, 8), every)] = zero8
-            for idx in lead_r:
-                R[b][idx + (p, pl.ds(0, 8), every)] = zero8
-                R[b][idx + (p, pl.ds(72, 8), every)] = zero8
-        return carry
-
-    lax.fori_loop(0, CX + 2, pads, 0)
-
-    def pads_u(p, carry):
-        for b in range(2):
-            for idx in lead_r:
-                U[b][idx + (p, pl.ds(0, 8), every)] = zero8
-                U[b][idx + (p, pl.ds(72, 8), every)] = zero8
-        return carry
-
-    lax.fori_loop(0, CU, pads_u, 0)
-
-    def to_col(row, n):
-        eye = lax.broadcasted_iota(jnp.int32, (n, n), 0) == lax.broadcasted_iota(
-            jnp.int32, (n, n), 1
-        )
-        return jnp.sum(jnp.where(eye, row, 0.0), axis=1, keepdims=True)
-
-    first_row = ((me_g * CX - HU) * NY).astype(f32)
-
-    def hot_rows(row, lo, n):
-        rows = lax.broadcasted_iota(jnp.int32, (n, REC), 0).astype(f32) + (first_row + lo)
-        rowhot[pl.ds(lo, n), :] = jnp.where(rows == row, 1.0, 0.0).astype(bf16)
-
-    lane_z = lax.broadcasted_iota(jnp.int32, (REC, NZ), 1).astype(f32)
-
-    def hot_z(z_row, g):
-        hot = jnp.where(lane_z == to_col(z_row, REC), 1.0, 0.0).astype(bf16)
-        zh2[g, pl.ds(0, REC), :] = hot
-        zh2[g, pl.ds(REC, REC), :] = hot
-
-    hot_rows(rec_row, HU * NY, CX * NY)
-    hot_z(rec_z, 1)
-    zt[...] = jnp.where(
-        lax.broadcasted_iota(jnp.int32, (NZ, REC), 0).astype(f32) == rec_z, 1.0, 0.0
-    ).astype(bf16)
 
     nx = n_gx * CX
     lane = lax.broadcasted_iota(jnp.int32, (8, HALF), 1)
@@ -450,36 +451,30 @@
                 for s in range(NS)
             )
 
-        got = lax.fori_loop(0, CX, one, (zero, zero), unroll=4)
+        got = lax.fori_loop(0, CX, one, (zero, zero), unroll=8)
         for s in range(NS):
             tr[pl.ds(s * STEPS + n, 1), :] = jnp.sum(got[s], axis=0, keepdims=True)
 
-    def inject(m, amounts, lo, hi):
-        nxt = U[m % 2]
-        n = STEPS - 1 - m
-
+    def inject(kind, lo, hi):
         def plane(i, carry):
             g = (i + CX - HU) // CX
             hot = rowhot[pl.ds(pl.multiple_of(i * NY, NY), NY), :].astype(f32)
-            parts = []
             for s in range(NS):
-                v = amounts[g, pl.ds(s * STEPS + n, 1), :]
-                v_hi = v.astype(bf16).astype(f32)
-                parts.append(
-                    jnp.concatenate(
-                        [(hot * v_hi).astype(bf16), (hot * (v - v_hi)).astype(bf16)], axis=1
+                parts = []
+                for n in range(STEPS):
+                    v = amt_s[kind, g, pl.ds(s * STEPS + n, 1), :]
+                    v_hi = v.astype(bf16).astype(f32)
+                    parts.append(
+                        jnp.concatenate(
+                            [(hot * v_hi).astype(bf16), (hot * (v - v_hi)).astype(bf16)], axis=1
+                        )
                     )
-                )
-            e = jnp.dot(jnp.concatenate(parts, axis=0), zh2[g], preferred_element_type=f32)
-            for s in range(NS):
-                for z in range(2):
-                    u = inv[z, i] * e[s * NY : (s + 1) * NY, z * HALF : (z + 1) * HALF]
-                    if m > 1:
-                        u = u - cb[z, i] * nxt[s, z, i, data, :]
-                    nxt[s, z, i, data, :] = u
+                e = jnp.dot(jnp.concatenate(parts, axis=0), zh2[g], preferred_element_type=f32)
+                for n in range(STEPS):
+                    E[s * STEPS + n, i] = e[n * NY : (n + 1) * NY]
             return carry
 
-        lax.fori_loop(lo, hi, plane, 0, unroll=2)
+        lax.fori_loop(lo, hi, plane, 0)
 
     def level(m, img):
         now, nxt = U[(m + 1) % 2], U[m % 2]
@@ -497,11 +492,14 @@
                     if m > 0:
                         mid, sums = neighbours(now, (s,), i, y8)
                     for z in range(2):
-                        u = nxt[s, z, i, ysp, :]
+                        zs = pl.ds(z * HALF, HALF)
+                        u = inv[z, i, ys, :] * E[s * STEPS + n, i, ys, zs]
                         if m > 0:
-                            u = u + ca[z, i, ys, :] * mid[z] + cc[z, i, ys, :] * sums[z]
-                            if m < STEPS - 1:
-                                nxt[s, z, i, ysp, :] = u
+                            u = u + (ca[z, i, ys, :] * mid[z] + cc[z, i, ys, :] * sums[z])
+                        if m > 1:
+                            u = u - cb[z, i, ys, :] * nxt[s, z, i, ysp, :]
+                        if m < STEPS - 1:
+                            nxt[s, z, i, ysp, :] = u
                         if image:
                             part = band[s, n, q, ys, pl.ds(z * HALF, HALF)] * u
                             pic[z] = part if s == 0 else pic[z] + part
@@ -515,50 +513,61 @@
             lax.fori_loop(0, 8, chunk, 0, unroll=8)
             return carry
 
-        if 0 < m < STEPS - 1:
+        if m < STEPS - 1:
             lax.fori_loop(m, HU, functools.partial(plane, False), 0)
             lax.fori_loop(HU + CX, CU - m, functools.partial(plane, False), 0)
-        lax.fori_loop(HU, HU + CX, functools.partial(plane, True), 0)
+        lax.fori_loop(HU, HU + CX, functools.partial(plane, True), 0, unroll=2)
+
+    def edge_bs(n):
+        def one(k, carry):
+            step_bs(n, 1 + (CX - 1) * k)
+            return carry
+
+        lax.fori_loop(0, 2, one, 0)
+
+    def edge_r(n):
+        def one(k, carry):
+            step_r(n, 1 + (CX - 1) * k)
+            return carry
+
+        lax.fori_loop(0, 2, one, 0)
+
+    def inner_bs(n):
+        def one(p, carry):
+            step_bs(n, p)
+            return carry
+
+        lax.fori_loop(2, CX, one, 0, unroll=2)
+
+    def inner_r(n):
+        def one(p, carry):
+            step_r(n, p)
+            return carry
+
+        lax.fori_loop(2, CX, one, 0, unroll=2)
 
     for n in range(STEPS):
-        bs_faces(n).wait_recv()
         if n == 0:
             wait_load("bs1")
+            inner_bs(n)
+            wait_load("r1")
+            inner_r(n)
+        bs_faces(n).wait_recv()
         if n > 0:
             bs_faces(n - 1).wait_send()
-
-        def edge_bs(k, carry):
-            step_bs(n, 1 + (CX - 1) * k)
-            return carry
-
-        lax.fori_loop(0, 2, edge_bs, 0)
+        edge_bs(n)
         if n < STEPS - 1:
             bs_faces(n + 1).start()
+        if n > 0:
+            inner_bs(n)
         r_faces(n).wait_recv()
-        if n == 0:
-            wait_load("r1")
         if n > 0:
             r_faces(n - 1).wait_send()
-
-        def edge_r(k, carry):
-            step_r(n, 1 + (CX - 1) * k)
-            return carry
-
-        lax.fori_loop(0, 2, edge_r, 0)
+        edge_r(n)
         if n < STEPS - 1:
             r_faces(n + 1).start()
-
-        def inner_bs(p, carry):
-            step_bs(n, p)
-            return carry
-
-        lax.fori_loop(2, CX, inner_bs, 0)
-
-        def inner_r(p, carry):
-            step_r(n, p)
-            return carry
-
-        lax.fori_loop(2, CX, inner_r, 0)
+        if n > 0:
+            inner_r(n)
         gather(n)
         if n == 0:
             info_halo.wait_recv()
@@ -571,7 +580,7 @@
             amt_s[0, 0] = info_n[0, pl.ds(0, 8), :]
             amt_s[0, 1] = info[pl.ds(0, 8), :]
             amt_s[0, 2] = info_n[1, pl.ds(0, 8), :]
-        inject(n, amt_s.at[0], n, CU - n)
+            inject(0, 0, CU)
         level(n, img_r)
     bs_faces(STEPS - 1).wait_send()
     r_faces(STEPS - 1).wait_send()
@@ -633,16 +642,15 @@
     tr_halo.start()
     sum_start(t * t, 0)
     amt_s[1, 1] = t
-    inject(0, amt_s.at[1], HU, HU + CX)
+    inject(1, HU, HU + CX)
     tr_halo.wait_recv()
     amt_s[1, 0] = tr_n[0]
     amt_s[1, 2] = tr_n[1]
-    inject(0, amt_s.at[1], 0, HU)
-    inject(0, amt_s.at[1], HU + CX, CU)
+    inject(1, 0, HU)
+    inject(1, HU + CX, CU)
     level(0, img_t)
     sum_middle(0)
     for m in range(1, STEPS):
-        inject(m, amt_s.at[1], m, CU - m)
         level(m, img_t)
     energy = sum_end(0)
     gn = jnp.full((8, HALF), grad_norm[0], f32)
@@ -724,18 +732,28 @@
         c.wait_send()
 
 
-def finish(scal, gradient, direction, model_image, resid, image_o, dir_o, resid_o):
+def finish(scal, gradient, direction, model_image, resid, image_o, dir_o, resid_o, image, out, sem):
     step = scal[0:1, 0:1]
     ratio = scal[8:9, 0:1]
-
-    def plane(p, carry):
-        d = direction[p]
-        image_o[p] = model_image[p] + step * d
-        dir_o[p] = gradient[p] + ratio * d
-        return carry
-
-    lax.fori_loop(0, CX, plane, 0)
-    resid_o[...] = resid[...]
+    copies = [pltpu.make_async_copy(resid, resid_o, sem.at[0])]
+    copies[0].start()
+    half = CX // 2
+    for k in range(2):
+        ps = pl.ds(k * half, half)
+
+        def plane(p, carry):
+            d = direction[p]
+            image[p] = model_image[p] + step * d
+            out[p] = gradient[p] + ratio * d
+            return carry
+
+        lax.fori_loop(k * half, (k + 1) * half, plane, 0)
+        for b, (src, dst) in enumerate(((image, image_o), (out, dir_o))):
+            c = pltpu.make_async_copy(src.at[ps], dst.at[ps], sem.at[1 + 2 * k + b])
+            c.start()
+            copies.append(c)
+    for c in copies:
+        c.wait()
 
 
 def per_device(
@@ -797,6 +815,7 @@
             V((NS * STEPS, REC), f32),
             V((2, NS * STEPS, REC), f32),
             V((2, 3, NS * STEPS, REC), f32),
+            V((NS * STEPS, CU, NY, NZ), f32),
             V((CX, NY, NZ), f32),
             V((CX, NY, NZ), f32),
             V((n_shot - 1, NY, NZ), f32),
@@ -842,13 +861,14 @@
     )
     return pl.pallas_call(
         finish,
-        out_shape=(
+        out_shape=[
             jax.ShapeDtypeStruct((CX, NY, NZ), f32),
             jax.ShapeDtypeStruct((CX, NY, NZ), f32),
             jax.ShapeDtypeStruct((NS, STEPS, REC), f32),
-        ),
+        ],
         in_specs=[vmem] * 5,
-        out_specs=(vmem, vmem, vmem),
+        out_specs=[pl.BlockSpec(memory_space=pltpu.HBM)] * 3,
+        scratch_shapes=[V((CX, NY, NZ), f32), V((CX, NY, NZ), f32), dma((5,))],
         compiler_params=pltpu.CompilerParams(vmem_limit_bytes=16 * 1024 * 1024),
         name="finish",
     )(scal, gradient, direction, model_image, resid)

time: 80.2 us -> 75.4 us (0.940)
  Pallas kernels: 75.7 us -> 71.4 us
    pallas_call x1, Pallas kernels: 74.4 us -> 70.2 us  [per_device(): pl.pallas_call(functools.partial(kernel, n_shot, n_gx), out_shape=(jax.Sh...]
where the time goes in v2:
time: 75.4 us; the launch traced here: 75.1 us
  Pallas kernels  71.4 us (95%)
  local copies, waits for them, and re-layouts  2.41 us (3%)
  between operations  1.33 us (2%)
    pallas_call x1, Pallas kernels, per_device(): pl.pallas_call(functools.partial(kernel, n_shot, n_gx), out_shape=(jax.Sh...  70.2 us
    unnamed x10, local copies, waits for them, and re-layouts  2.41 us

profile of v2, /device:TPU:1, one launch (start us, length us, event | category | flops | bytes accessed | tf_op | source)
XLA Modules:
  0.0 75.1 jit_solution(13800145207940446124)
XLA Ops:
  1.3 0.0 copy-start
  1.3 0.0 copy-start.1
  1.3 70.2 %lsrtm.1 = (f32[8,64,256]{2,1,0:T(8,128)}, f32[2,4,128]{2,1,0:T(4,128)}, f32[16,128]{1,0:T(8,128)}) custom-call(f32[8,64,256]{2,1,0:T(8,128)} %courant_h.1, f32[8,64,256]{2,1,0:T(8,128)} %direction.1, f32[2,8,64,256]{3,2,1,0:T(8,128)} %back_prev_h.1, f32[2,8,64,256]{3,2,1,0:T(8,128)} %back_now_h.1, f32[2,8,64,256]{3,2,1,0:T(8,128)} %scat_prev_h.1, ...), custom_call_target="tpu_custom_call" | custom-call | tf_op jit(solution)/shard_map/lsrtm/pallas_call | solution.py:786
  71.5 0.0 copy-done
  71.5 0.0 copy-done.1
  71.5 0.0 copy-start.2
  71.5 1.0 %copy-done.2 = f32[8,64,256]{2,1,0:T(8,128)S(1)} copy-done((f32[8,64,256]{2,1,0:T(8,128)S(1)}, f32[8,64,256]{2,1,0:T(8,128)}, u32[]{:S(2)}) %copy-start.2) | copy-done | bytes 524312
  72.6 0.0 copy-start.3
  72.6 0.7 copy-done.3
  73.3 0.0 copy-start.4
  73.3 0.7 copy-done.4
  74.0 1.2 %finish.1 = (f32[8,64,256]{2,1,0:T(8,128)}, f32[8,64,256]{2,1,0:T(8,128)}, f32[2,4,128]{2,1,0:T(4,128)}) custom-call(f32[16,128]{1,0:T(8,128)S(1)} %copy-done.3, f32[8,64,256]{2,1,0:T(8,128)S(1)} %copy-done.2, f32[8,64,256]{2,1,0:T(8,128)S(1)} %copy-done, f32[8,64,256]{2,1,0:T(8,128)S(1)} %copy-done.1, f32[2,4,128]{2,1,0:T(4,128)S(1)} %copy-done.4), custom_call_target="tpu_custom_call" | custom-call | tf_op jit(solution)/shard_map/finish/pallas_call | solution.py:862
Async XLA Ops:
  1.3 70.2 %copy-start = (f32[8,64,256]{2,1,0:T(8,128)S(1)}, f32[8,64,256]{2,1,0:T(8,128)}, u32[]{:S(2)}) copy-start(f32[8,64,256]{2,1,0:T(8,128)} %direction.1) | copy-start | bytes 1572868
  1.3 70.2 %copy-start.1 = (f32[8,64,256]{2,1,0:T(8,128)S(1)}, f32[8,64,256]{2,1,0:T(8,128)}, u32[]{:S(2)}) copy-start(f32[8,64,256]{2,1,0:T(8,128)} %model_image.1) | copy-start | bytes 1572868
  71.5 1.0 %copy-start.2 = (f32[8,64,256]{2,1,0:T(8,128)S(1)}, f32[8,64,256]{2,1,0:T(8,128)}, u32[]{:S(2)}) copy-start(f32[8,64,256]{2,1,0:T(8,128)} %get-tuple-element.7.gradient) | copy-start | bytes 1572868
  72.6 0.7 copy-start.3
  73.3 0.7 copy-start.4

commit v3 on v2

--- a/solution.py
+++ b/solution.py
@@ -223,13 +223,13 @@
     def face(buf, lead, p):
         return buf.at[(every,) * lead + (p, data, every)]
 
-    def bs_faces(n):
+    def bs_faces(n, s):
         b = F[n % 2]
         return Pair(
-            (face(b, 3, 1), face(b, 3, CX + 1)),
-            (face(b, 3, CX), face(b, 3, 0)),
-            f_send.at[n],
-            f_recv.at[n],
+            (b.at[:, s, :, 1, data, :], b.at[:, s, :, CX + 1, data, :]),
+            (b.at[:, s, :, CX, data, :], b.at[:, s, :, 0, data, :]),
+            f_send.at[n, s],
+            f_recv.at[n, s],
         )
 
     def r_faces(n):
@@ -299,7 +299,8 @@
     pl.semaphore_wait(bar, n_gx - 1 + n_shot - 1)
     wait_load("b0")
     wait_load("s0")
-    bs_faces(0).start()
+    for s in range(NS):
+        bs_faces(0, s).start()
     wait_load("r0")
     r_faces(0).start()
     info_halo.start()
@@ -371,7 +372,7 @@
             sums.append(t + (low[z] + high[z]))
         return mid, sums
 
-    def step_bs(n, p):
+    def step_bs(n, p, shots):
         now, nxt = F[n % 2], F[(n + 1) % 2]
         q = p - 1
         i = q + HU
@@ -384,7 +385,7 @@
             b = [cb[z, i, ys, :] for z in range(2)]
             c = [cc[z, i, ys, :] for z in range(2)]
             di = [dirv[z, q, ys, :] for z in range(2)]
-            for s in range(NS):
+            for s in shots:
                 w = wavelet[s, n]
                 mid, sums = neighbours(now, (0, s), p, y8)
                 acc = []
@@ -518,12 +519,12 @@
             lax.fori_loop(HU + CX, CU - m, functools.partial(plane, False), 0)
         lax.fori_loop(HU, HU + CX, functools.partial(plane, True), 0, unroll=2)
 
-    def edge_bs(n):
+    def edge_bs(n, s):
         def one(k, carry):
-            step_bs(n, 1 + (CX - 1) * k)
+            step_bs(n, 1 + (CX - 1) * k, (s,))
             return carry
 
-        lax.fori_loop(0, 2, one, 0)
+        lax.fori_loop(0, 2, one, 0, unroll=2)
 
     def edge_r(n):
         def one(k, carry):
@@ -532,9 +533,9 @@
 
         lax.fori_loop(0, 2, one, 0)
 
-    def inner_bs(n):
+    def inner_bs(n, shots):
         def one(p, carry):
-            step_bs(n, p)
+            step_bs(n, p, shots)
             return carry
 
         lax.fori_loop(2, CX, one, 0, unroll=2)
@@ -549,17 +550,18 @@
     for n in range(STEPS):
         if n == 0:
             wait_load("bs1")
-            inner_bs(n)
+            inner_bs(n, range(NS))
             wait_load("r1")
             inner_r(n)
-        bs_faces(n).wait_recv()
-        if n > 0:
-            bs_faces(n - 1).wait_send()
-        edge_bs(n)
-        if n < STEPS - 1:
-            bs_faces(n + 1).start()
-        if n > 0:
-            inner_bs(n)
+        for s in range(NS):
+            bs_faces(n, s).wait_recv()
+            if n > 0:
+                bs_faces(n - 1, s).wait_send()
+            edge_bs(n, s)
+            if n < STEPS - 1:
+                bs_faces(n + 1, s).start()
+            if n > 0:
+                inner_bs(n, (s,))
         r_faces(n).wait_recv()
         if n > 0:
             r_faces(n - 1).wait_send()
@@ -582,15 +584,29 @@
             amt_s[0, 2] = info_n[1, pl.ds(0, 8), :]
             inject(0, 0, CU)
         level(n, img_r)
-    bs_faces(STEPS - 1).wait_send()
+    for s in range(NS):
+        bs_faces(STEPS - 1, s).wait_send()
     r_faces(STEPS - 1).wait_send()
     info_halo.wait_send()
     c_halo.wait_send()
 
+    def to_slabs(r):
+        return [
+            pltpu.make_async_remote_copy(
+                src_ref=ebuf.at[r, 0],
+                dst_ref=eslot_g.at[r, me_g],
+                send_sem=e_send_g.at[r, d],
+                recv_sem=e_recv_g.at[r, d],
+                device_id=(me_s, lax.rem(me_g + d, n_gx)),
+                device_id_type=MESH,
+            )
+            for d in range(1, n_gx)
+        ]
+
     def to_shots(r):
         return [
             pltpu.make_async_remote_copy(
-                src_ref=ebuf.at[r, 0],
+                src_ref=ebuf.at[r, 1],
                 dst_ref=eslot_s.at[r, me_s],
                 send_sem=e_send_s.at[r, d],
                 recv_sem=e_recv_s.at[r, d],
@@ -600,42 +616,29 @@
             for d in range(1, n_shot)
         ]
 
-    def to_slabs(r):
-        return [
-            pltpu.make_async_remote_copy(
-                src_ref=ebuf.at[r, 1],
-                dst_ref=eslot_g.at[r, me_g],
-                send_sem=e_send_g.at[r, d],
-                recv_sem=e_recv_g.at[r, d],
-                device_id=(me_s, lax.rem(me_g + d, n_gx)),
-                device_id_type=MESH,
-            )
-            for d in range(1, n_gx)
-        ]
-
     def sum_start(value, r):
         ebuf[r, 0] = value
-        eslot_s[r, me_s] = value
+        eslot_g[r, me_g] = value
+        for c in to_slabs(r):
+            c.start()
+
+    def sum_middle(r):
+        for c in to_slabs(r):
+            c.wait_recv()
+        total = eslot_g[r, 0]
+        for d in range(1, n_gx):
+            total = total + eslot_g[r, d]
+        ebuf[r, 1] = total
+        eslot_s[r, me_s] = total
         for c in to_shots(r):
             c.start()
 
-    def sum_middle(r):
+    def sum_end(r):
         for c in to_shots(r):
             c.wait_recv()
         total = eslot_s[r, 0]
         for d in range(1, n_shot):
             total = total + eslot_s[r, d]
-        ebuf[r, 1] = total
-        eslot_g[r, me_g] = total
-        for c in to_slabs(r):
-            c.start()
-
-    def sum_end(r):
-        for c in to_slabs(r):
-            c.wait_recv()
-        total = eslot_g[r, 0]
-        for d in range(1, n_gx):
-            total = total + eslot_g[r, d]
         return jnp.sum(total)
 
     t = tr[...]
@@ -650,7 +653,7 @@
     inject(1, HU + CX, CU)
     level(0, img_t)
     sum_middle(0)
-    for m in range(1, STEPS):
+    for m in range(1, STEPS - 1):
         level(m, img_t)
     energy = sum_end(0)
     gn = jnp.full((8, HALF), grad_norm[0], f32)
@@ -658,20 +661,9 @@
     for s in range(NS):
         resid_o[s] = residual[s] - step[0:STEPS] * t[s * STEPS : (s + 1) * STEPS]
 
-    def combine(q):
-        for y in range(8):
-            ys = pl.ds(y * 8, 8)
-            for z in range(2):
-                zs = pl.ds(z * HALF, HALF)
-                img_r[q, ys, zs] = c0[z, HU + q, ys, :] * (
-                    step * img_t[q, ys, zs] - img_r[q, ys, zs]
-                )
-
-    scatter = []
-    for d in range(1, n_shot):
+    def to_sum(d):
         to = lax.rem(me_s + d, n_shot)
-        combine(to)
-        c = pltpu.make_async_remote_copy(
+        return pltpu.make_async_remote_copy(
             src_ref=img_r.at[to],
             dst_ref=rs.at[d - 1],
             send_sem=g_send.at[0, d],
@@ -679,11 +671,43 @@
             device_id=(to, me_g),
             device_id_type=MESH,
         )
-        c.start()
-        scatter.append(c)
-    combine(me_s)
-    for c in scatter:
-        c.wait_recv()
+
+    m_last = STEPS - 1
+    now_u, old_u = U[(m_last + 1) % 2], U[m_last % 2]
+
+    def gradient_plane(d, carry):
+        q = lax.rem(me_s + d, n_shot)
+        i = q + HU
+
+        def chunk(j, inner):
+            y8 = pl.multiple_of(j * 8, 8)
+            ys = pl.ds(y8, 8)
+            ysp = pl.ds(pl.multiple_of(y8 + 8, 8), 8)
+            pic = [img_t[q, ys, pl.ds(z * HALF, HALF)] for z in range(2)]
+            for s in range(NS):
+                mid, sums = neighbours(now_u, (s,), i, y8)
+                for z in range(2):
+                    zs = pl.ds(z * HALF, HALF)
+                    u = inv[z, i, ys, :] * E[s * STEPS, i, ys, zs]
+                    u = u + (ca[z, i, ys, :] * mid[z] + cc[z, i, ys, :] * sums[z])
+                    u = u - cb[z, i, ys, :] * old_u[s, z, i, ysp, :]
+                    pic[z] = pic[z] + band[s, 0, q, ys, zs] * u
+            for z in range(2):
+                zs = pl.ds(z * HALF, HALF)
+                img_r[q, ys, zs] = c0[z, i, ys, :] * (step * pic[z] - img_r[q, ys, zs])
+            return inner
+
+        lax.fori_loop(0, 8, chunk, 0, unroll=8)
+
+        @pl.when(d < n_shot)
+        def _():
+            to_sum(d).start()
+
+        return carry
+
+    lax.fori_loop(1, n_shot + 1, gradient_plane, 0)
+    for d in range(1, n_shot):
+        to_sum(d).wait_recv()
 
     def add(i, carry):
         ys = pl.ds(pl.multiple_of(i * 8, 8), 8)
@@ -696,20 +720,21 @@
 
     part = lax.fori_loop(0, 8, add, jnp.zeros((8, HALF), f32), unroll=8)
     sum_start(part, 1)
-    spread = []
-    for d in range(1, n_shot):
-        to = lax.rem(me_s + d, n_shot)
-        c = pltpu.make_async_remote_copy(
+    def spread(d):
+        return pltpu.make_async_remote_copy(
             src_ref=grad_o.at[me_s],
             dst_ref=grad_o.at[me_s],
             send_sem=g_send.at[1, d],
             recv_sem=g_recv.at[1, d],
-            device_id=(to, me_g),
+            device_id=(lax.rem(me_s + d, n_shot), me_g),
             device_id_type=MESH,
         )
-        c.start()
-        spread.append(c)
+
+    for d in range(1, n_shot, 2):
+        spread(d).start()
     sum_middle(1)
+    for d in range(2, n_shot, 2):
+        spread(d).start()
     grad_energy = sum_end(1)
     ratio = jnp.full((8, HALF), grad_energy, f32) / gn
     scal_o[pl.ds(0, 8), :] = step
@@ -728,8 +753,9 @@
     for r in range(2):
         for c in to_shots(r) + to_slabs(r):
             c.wait_send()
-    for c in scatter + spread:
-        c.wait_send()
+    for d in range(1, n_shot):
+        to_sum(d).wait_send()
+        spread(d).wait_send()
 
 
 def finish(scal, gradient, direction, model_image, resid, image_o, dir_o, resid_o, image, out, sem):
@@ -823,8 +849,8 @@
             V((2, n_shot, 8, HALF), f32),
             V((2, n_gx, 8, HALF), f32),
             dma((17,)),
-            dma((STEPS, 2)),
-            dma((STEPS, 2)),
+            dma((STEPS, NS, 2)),
+            dma((STEPS, NS, 2)),
             dma((STEPS, 2)),
             dma((STEPS, 2)),
             dma((3, 2)),

time: 75.4 us -> 73.7 us (0.977)
  Pallas kernels: 71.4 us -> 69.4 us
    pallas_call x1, Pallas kernels: 70.2 us -> 68.2 us  [per_device(): pl.pallas_call(functools.partial(kernel, n_shot, n_gx), out_shape=(jax.Sh...]
where the time goes in v3:
time: 73.7 us; the launch traced here: 73.1 us
  Pallas kernels  69.4 us (94%)
  local copies, waits for them, and re-layouts  2.41 us (3%)
  between operations  1.33 us (2%)
    pallas_call x1, Pallas kernels, per_device(): pl.pallas_call(functools.partial(kernel, n_shot, n_gx), out_shape=(jax.Sh...  68.2 us
    unnamed x10, local copies, waits for them, and re-layouts  2.41 us

profile of v3, /device:TPU:1, one launch (start us, length us, event | category | flops | bytes accessed | tf_op | source)
XLA Modules:
  0.0 73.1 jit_solution(14770771997304671002)
XLA Ops:
  1.3 0.0 copy-start
  1.3 0.0 copy-start.1
  1.3 68.2 %lsrtm.1 = (f32[8,64,256]{2,1,0:T(8,128)}, f32[2,4,128]{2,1,0:T(4,128)}, f32[16,128]{1,0:T(8,128)}) custom-call(f32[8,64,256]{2,1,0:T(8,128)} %courant_h.1, f32[8,64,256]{2,1,0:T(8,128)} %direction.1, f32[2,8,64,256]{3,2,1,0:T(8,128)} %back_prev_h.1, f32[2,8,64,256]{3,2,1,0:T(8,128)} %back_now_h.1, f32[2,8,64,256]{3,2,1,0:T(8,128)} %scat_prev_h.1, ...), custom_call_target="tpu_custom_call" | custom-call | tf_op jit(solution)/shard_map/lsrtm/pallas_call | solution.py:812
  69.5 0.0 copy-done
  69.5 0.0 copy-done.1
  69.5 0.0 copy-start.2
  69.5 1.0 %copy-done.2 = f32[8,64,256]{2,1,0:T(8,128)S(1)} copy-done((f32[8,64,256]{2,1,0:T(8,128)S(1)}, f32[8,64,256]{2,1,0:T(8,128)}, u32[]{:S(2)}) %copy-start.2) | copy-done | bytes 524312
  70.6 0.0 copy-start.3
  70.6 0.7 copy-done.3
  71.3 0.0 copy-start.4
  71.3 0.7 copy-done.4
  72.0 1.2 %finish.1 = (f32[8,64,256]{2,1,0:T(8,128)}, f32[8,64,256]{2,1,0:T(8,128)}, f32[2,4,128]{2,1,0:T(4,128)}) custom-call(f32[16,128]{1,0:T(8,128)S(1)} %copy-done.3, f32[8,64,256]{2,1,0:T(8,128)S(1)} %copy-done.2, f32[8,64,256]{2,1,0:T(8,128)S(1)} %copy-done, f32[8,64,256]{2,1,0:T(8,128)S(1)} %copy-done.1, f32[2,4,128]{2,1,0:T(4,128)S(1)} %copy-done.4), custom_call_target="tpu_custom_call" | custom-call | tf_op jit(solution)/shard_map/finish/pallas_call | solution.py:888
Async XLA Ops:
  1.3 68.2 %copy-start = (f32[8,64,256]{2,1,0:T(8,128)S(1)}, f32[8,64,256]{2,1,0:T(8,128)}, u32[]{:S(2)}) copy-start(f32[8,64,256]{2,1,0:T(8,128)} %direction.1) | copy-start | bytes 1572868
  1.3 68.2 %copy-start.1 = (f32[8,64,256]{2,1,0:T(8,128)S(1)}, f32[8,64,256]{2,1,0:T(8,128)}, u32[]{:S(2)}) copy-start(f32[8,64,256]{2,1,0:T(8,128)} %model_image.1) | copy-start | bytes 1572868
  69.5 1.0 %copy-start.2 = (f32[8,64,256]{2,1,0:T(8,128)S(1)}, f32[8,64,256]{2,1,0:T(8,128)}, u32[]{:S(2)}) copy-start(f32[8,64,256]{2,1,0:T(8,128)} %get-tuple-element.7.gradient) | copy-start | bytes 1572868
  70.6 0.7 copy-start.3
  71.3 0.7 copy-start.4

commit v4 on v3

--- a/solution.py
+++ b/solution.py
@@ -54,8 +54,7 @@
     rec_pos,
     residual,
     grad_o,
-    resid_o,
-    scal_o,
+    aux_o,
     F0,
     F1,
     R0,
@@ -659,7 +658,9 @@
     gn = jnp.full((8, HALF), grad_norm[0], f32)
     step = gn / (jnp.full((8, HALF), energy, f32) + tiny)
     for s in range(NS):
-        resid_o[s] = residual[s] - step[0:STEPS] * t[s * STEPS : (s + 1) * STEPS]
+        aux_o[pl.ds(s * STEPS, STEPS), :] = (
+            residual[s] - step[0:STEPS] * t[s * STEPS : (s + 1) * STEPS]
+        )
 
     def to_sum(d):
         to = lax.rem(me_s + d, n_shot)
@@ -737,8 +738,8 @@
         spread(d).start()
     grad_energy = sum_end(1)
     ratio = jnp.full((8, HALF), grad_energy, f32) / gn
-    scal_o[pl.ds(0, 8), :] = step
-    scal_o[pl.ds(8, 8), :] = ratio
+    aux_o[pl.ds(8, 8), :] = step
+    aux_o[pl.ds(16, 8), :] = ratio
     for d in range(1, n_shot):
         came = lax.rem(me_s + n_shot - d, n_shot)
         pltpu.make_async_remote_copy(
@@ -758,27 +759,46 @@
         spread(d).wait_send()
 
 
-def finish(scal, gradient, direction, model_image, resid, image_o, dir_o, resid_o, image, out, sem):
-    step = scal[0:1, 0:1]
-    ratio = scal[8:9, 0:1]
-    copies = [pltpu.make_async_copy(resid, resid_o, sem.at[0])]
-    copies[0].start()
+def finish(
+    aux_h, gradient_h, direction_h, model_h, image_o, dir_o, resid_o,
+    aux, gradient, direction, image, resid, sem,
+):
     half = CX // 2
+    first = pltpu.make_async_copy(aux_h, aux, sem.at[0])
+    first.start()
+    come = []
     for k in range(2):
         ps = pl.ds(k * half, half)
+        for b, (src, dst) in enumerate(
+            ((gradient_h, gradient), (direction_h, direction), (model_h, image))
+        ):
+            c = pltpu.make_async_copy(src.at[ps], dst.at[ps], sem.at[1 + 3 * k + b])
+            c.start()
+            come.append(c)
+    first.wait()
+    step = aux[8:9, 0:1]
+    ratio = aux[16:17, 0:1]
+    for s in range(NS):
+        resid[s] = aux[s * STEPS : (s + 1) * STEPS, :]
+    gone = [pltpu.make_async_copy(resid, resid_o, sem.at[7])]
+    gone[0].start()
+    for k in range(2):
+        ps = pl.ds(k * half, half)
+        for c in come[3 * k : 3 * k + 3]:
+            c.wait()
 
         def plane(p, carry):
             d = direction[p]
-            image[p] = model_image[p] + step * d
-            out[p] = gradient[p] + ratio * d
+            image[p] = image[p] + step * d
+            gradient[p] = gradient[p] + ratio * d
             return carry
 
         lax.fori_loop(k * half, (k + 1) * half, plane, 0)
-        for b, (src, dst) in enumerate(((image, image_o), (out, dir_o))):
-            c = pltpu.make_async_copy(src.at[ps], dst.at[ps], sem.at[1 + 2 * k + b])
+        for b, (src, dst) in enumerate(((image, image_o), (gradient, dir_o))):
+            c = pltpu.make_async_copy(src.at[ps], dst.at[ps], sem.at[8 + 2 * k + b])
             c.start()
-            copies.append(c)
-    for c in copies:
+            gone.append(c)
+    for c in gone:
         c.wait()
 
 
@@ -809,15 +829,14 @@
     wide = (2, CU, NY, HALF)
     dma = pltpu.SemaphoreType.DMA
     V = pltpu.VMEM
-    gradient, resid, scal = pl.pallas_call(
+    gradient, aux = pl.pallas_call(
         functools.partial(kernel, n_shot, n_gx),
         out_shape=(
             jax.ShapeDtypeStruct((CX, NY, NZ), f32),
-            jax.ShapeDtypeStruct((NS, STEPS, REC), f32),
-            jax.ShapeDtypeStruct((16, HALF), f32),
+            jax.ShapeDtypeStruct((24, HALF), f32),
         ),
         in_specs=[hbm] * 9 + [smem] * 3 + [vmem] * 3,
-        out_specs=(vmem, vmem, vmem),
+        out_specs=(vmem, vmem),
         scratch_shapes=[
             V((2, NS, 2, CX + 2, PY, HALF), f32),
             V((2, NS, 2, CX + 2, PY, HALF), f32),
@@ -892,12 +911,19 @@
             jax.ShapeDtypeStruct((CX, NY, NZ), f32),
             jax.ShapeDtypeStruct((NS, STEPS, REC), f32),
         ],
-        in_specs=[vmem] * 5,
+        in_specs=[hbm] * 4,
         out_specs=[pl.BlockSpec(memory_space=pltpu.HBM)] * 3,
-        scratch_shapes=[V((CX, NY, NZ), f32), V((CX, NY, NZ), f32), dma((5,))],
-        compiler_params=pltpu.CompilerParams(vmem_limit_bytes=16 * 1024 * 1024),
+        scratch_shapes=[
+            V((24, HALF), f32),
+            V((CX, NY, NZ), f32),
+            V((CX, NY, NZ), f32),
+            V((CX, NY, NZ), f32),
+            V((NS, STEPS, REC), f32),
+            dma((12,)),
+        ],
+        compiler_params=pltpu.CompilerParams(vmem_limit_bytes=62 * 1024 * 1024),
         name="finish",
-    )(scal, gradient, direction, model_image, resid)
+    )(aux, gradient, direction, model_image)
 
 
 def solution(mesh):

time: 73.7 us -> 72.3 us (0.981)
  local copies, waits for them, and re-layouts: 2.41 us -> 0 us
  Pallas kernels: 69.4 us -> 70.6 us
    unnamed x10 -> x0, local copies, waits for them, and re-layouts: 2.41 us -> none
    pallas_call x1, Pallas kernels: 1.18 us -> 2.37 us  [per_device(): pl.pallas_call(finish, out_shape=[jax.ShapeDtypeStruct((CX, NY, NZ), f32)...]
where the time goes in v4:
time: 72.3 us; the launch traced here: 71.9 us
  Pallas kernels  70.6 us (98%)
  between operations  1.29 us (2%)
    pallas_call x1, Pallas kernels, per_device(): pl.pallas_call(functools.partial(kernel, n_shot, n_gx), out_shape=(jax.Sh...  68.2 us
    pallas_call x1, Pallas kernels, per_device(): pl.pallas_call(finish, out_shape=[jax.ShapeDtypeStruct((CX, NY, NZ), f32)...  2.37 us

profile of v4, /device:TPU:1, one launch (start us, length us, event | category | flops | bytes accessed | tf_op | source)
XLA Modules:
  0.0 71.9 jit_solution(4407149235825560544)
XLA Ops:
  1.3 68.2 %lsrtm.1 = (f32[8,64,256]{2,1,0:T(8,128)}, f32[24,128]{1,0:T(8,128)}) custom-call(f32[8,64,256]{2,1,0:T(8,128)} %courant_h.1, f32[8,64,256]{2,1,0:T(8,128)} %direction_h.3, f32[2,8,64,256]{3,2,1,0:T(8,128)} %back_prev_h.1, f32[2,8,64,256]{3,2,1,0:T(8,128)} %back_now_h.1, f32[2,8,64,256]{3,2,1,0:T(8,128)} %scat_prev_h.1, f32[2,8,64,256]{3,2,1,0:T(8,128)} %scat_now_h.1, ...), custom_call_target="tpu_custom_call" | custom-call | tf_op jit(solution)/shard_map/lsrtm/pallas_call | solution.py:832
  69.5 2.4 %finish.1 = (f32[8,64,256]{2,1,0:T(8,128)}, f32[8,64,256]{2,1,0:T(8,128)}, f32[2,4,128]{2,1,0:T(4,128)}) custom-call(f32[24,128]{1,0:T(8,128)} %get-tuple-element.5.aux_h, f32[8,64,256]{2,1,0:T(8,128)} %get-tuple-element.6.gradient_h, f32[8,64,256]{2,1,0:T(8,128)} %direction_h.3, f32[8,64,256]{2,1,0:T(8,128)} %model_h.1), custom_call_target="tpu_custom_call" | custom-call | tf_op jit(solution)/shard_map/finish/pallas_call | solution.py:907

commit v5 on v4

--- a/solution.py
+++ b/solution.py
@@ -474,7 +474,7 @@
                     E[s * STEPS + n, i] = e[n * NY : (n + 1) * NY]
             return carry
 
-        lax.fori_loop(lo, hi, plane, 0)
+        lax.fori_loop(lo, hi, plane, 0, unroll=2)
 
     def level(m, img):
         now, nxt = U[(m + 1) % 2], U[m % 2]
@@ -530,7 +530,7 @@
             step_r(n, 1 + (CX - 1) * k)
             return carry
 
-        lax.fori_loop(0, 2, one, 0)
+        lax.fori_loop(0, 2, one, 0, unroll=2)
 
     def inner_bs(n, shots):
         def one(p, carry):

time: 72.3 us -> 69.8 us (0.965)
  Pallas kernels: 70.6 us -> 68.4 us
    pallas_call x1, Pallas kernels: 68.2 us -> 66 us  [per_device(): pl.pallas_call(functools.partial(kernel, n_shot, n_gx), out_shape=(jax.Sh...]
where the time goes in v5:
time: 69.8 us; the launch traced here: 69.7 us
  Pallas kernels  68.4 us (98%)
  between operations  1.29 us (2%)
    pallas_call x1, Pallas kernels, per_device(): pl.pallas_call(functools.partial(kernel, n_shot, n_gx), out_shape=(jax.Sh...  66 us
    pallas_call x1, Pallas kernels, per_device(): pl.pallas_call(finish, out_shape=[jax.ShapeDtypeStruct((CX, NY, NZ), f32)...  2.37 us

profile of v5, /device:TPU:1, one launch (start us, length us, event | category | flops | bytes accessed | tf_op | source)
XLA Modules:
  0.0 69.7 jit_solution(410105084651029866)
XLA Ops:
  1.3 66.0 %lsrtm.1 = (f32[8,64,256]{2,1,0:T(8,128)}, f32[24,128]{1,0:T(8,128)}) custom-call(f32[8,64,256]{2,1,0:T(8,128)} %courant_h.1, f32[8,64,256]{2,1,0:T(8,128)} %direction_h.3, f32[2,8,64,256]{3,2,1,0:T(8,128)} %back_prev_h.1, f32[2,8,64,256]{3,2,1,0:T(8,128)} %back_now_h.1, f32[2,8,64,256]{3,2,1,0:T(8,128)} %scat_prev_h.1, f32[2,8,64,256]{3,2,1,0:T(8,128)} %scat_now_h.1, ...), custom_call_target="tpu_custom_call" | custom-call | tf_op jit(solution)/shard_map/lsrtm/pallas_call | solution.py:832
  67.3 2.4 %finish.1 = (f32[8,64,256]{2,1,0:T(8,128)}, f32[8,64,256]{2,1,0:T(8,128)}, f32[2,4,128]{2,1,0:T(4,128)}) custom-call(f32[24,128]{1,0:T(8,128)} %get-tuple-element.5.aux_h, f32[8,64,256]{2,1,0:T(8,128)} %get-tuple-element.6.gradient_h, f32[8,64,256]{2,1,0:T(8,128)} %direction_h.3, f32[8,64,256]{2,1,0:T(8,128)} %model_h.1), custom_call_target="tpu_custom_call" | custom-call | tf_op jit(solution)/shard_map/finish/pallas_call | solution.py:907
